TPU v7x, 32 devices: a whole 2x2x4 slice. The times are simulated.
32 devices in a mesh: row: 8 (over z, core), col: 4 (over y, x).
Axes of the slice: x: 2, y: 2, z: 4, core: 2. Of those that a mesh axis runs over, the one named last changes fastest.
Arguments:
- patches: bfloat16 [256, 256, 256], P('row', 'col'), may hold values from -6 to 6
- norm_gain: float32 [256], replicated, may hold values from 0.1 to 1.9
- w_first: bfloat16 [2, 4, 64, 64], replicated, may hold values from -0.5 to 0.5
- w_second: bfloat16 [2, 4, 64, 64], replicated, may hold values from -0.5 to 0.5
- depth_kernel: float32 [3, 3, 256], replicated, may hold values from -2 to 2
Outputs:
- mixed: bfloat16 [256, 256, 256], P('row', 'col')
All inputs are finite; a program needn't handle non-finite values.
Results may differ from a plain program's by a relative error of at most 0.008.
Values may be sent and summed in bfloat16 or wider, within the bound.
A program may use at most 64 MiB of HBM per device.

v0:
```python
import math

import jax
import jax.numpy as jnp
from jax import lax
from jax.sharding import PartitionSpec as P


def with_halo(shard, sides, width):
    for axis, dim in sides:
        devices, length = (lax.axis_size(axis), shard.shape[dim])
        up = [(i, (i + 1) % devices) for i in range(devices)]
        down = [(j, i) for i, j in up]
        last = lax.slice_in_dim(shard, length - width, length, axis=dim)
        leading = lax.slice_in_dim(shard, 0, width, axis=dim)
        before = lax.ppermute(last, axis, up)
        after = lax.ppermute(leading, axis, down)
        shard = jnp.concatenate([before, shard, after], axis=dim)
    return shard


def phase_table(first_idx, second_idx, length):
    product = first_idx[:, None] * second_idx[None, :] % length
    phase = product.astype(jnp.float32) * (2.0 * math.pi / length)
    return (jnp.cos(phase).astype(jnp.bfloat16), jnp.sin(phase).astype(jnp.bfloat16))


def shrink(values):
    level = 0.25
    return jnp.where(
        values > level, values - level, jnp.where(values < -level, values + level, 0.0 * values)
    )


def block_product(left, weight):
    return jnp.einsum("qmbc,bcd->qmbd", left, weight, preferred_element_type=jnp.float32)


def local(patches, norm_gain, w_first, w_second, depth_kernel):
    n_row = lax.axis_size("row")
    n_col = lax.axis_size("col")
    rows_dev, cols_dev, chans = patches.shape
    patch_grid_height = rows_dev * n_row
    grid_w = cols_dev * n_col
    half = grid_w // 2
    blocks = w_first.shape[1]
    width = w_first.shape[2]
    width_factors = 1.0 / math.sqrt(grid_w)
    height_factors = 1.0 / math.sqrt(patch_grid_height)
    xf = patches.astype(jnp.float32)
    mean = jnp.mean(xf, axis=-1, keepdims=True)
    var = jnp.mean((xf - mean) ** 2, axis=-1, keepdims=True)
    normed = ((xf - mean) * lax.rsqrt(var + 1e-05) * norm_gain).astype(jnp.bfloat16)
    padded = with_halo(normed, (("row", 0), ("col", 1)), 1)
    conv = jnp.zeros((rows_dev, cols_dev, chans), jnp.float32)
    for i in range(3):
        for j in range(3):
            conv = conv + padded[i : i + rows_dev, j : j + cols_dev] * depth_kernel[i, j]
    strips = lax.all_to_all(normed, "col", split_axis=0, concat_axis=1, tiled=True)
    cos_w, sin_w = phase_table(
        jnp.arange(grid_w, dtype=jnp.int32), jnp.arange(half, dtype=jnp.int32), grid_w
    )
    forward_w = jnp.concatenate([cos_w, -sin_w], axis=1)
    spectrum_values = jnp.einsum(
        "hwc,wk->hkc", strips, forward_w, preferred_element_type=jnp.float32
    )
    spectrum_values = (spectrum_values * width_factors).astype(jnp.bfloat16)
    wre = spectrum_values[:, :half]
    wim = spectrum_values[:, half:]
    positions = jnp.arange(patch_grid_height, dtype=jnp.int32)
    across_re, across_im = (
        lax.all_to_all(wre, "col", split_axis=1, concat_axis=0, tiled=True),
        lax.all_to_all(wim, "col", split_axis=1, concat_axis=0, tiled=True),
    )
    full_re, full_im = (
        lax.all_to_all(across_re, "row", split_axis=1, concat_axis=0, tiled=True),
        lax.all_to_all(across_im, "row", split_axis=1, concat_axis=0, tiled=True),
    )
    cos_h, sin_h = phase_table(positions, positions, patch_grid_height)
    big_table = jnp.concatenate(
        [jnp.concatenate([cos_h, sin_h], axis=1), jnp.concatenate([-sin_h, cos_h], axis=1)], axis=0
    )
    stacked = jnp.concatenate([full_re, full_im], axis=0)
    spectrum = jnp.einsum("qp,pmc->qmc", big_table, stacked, preferred_element_type=jnp.float32)
    spectrum = (spectrum * height_factors).astype(jnp.bfloat16)
    modes = spectrum.shape[1]
    zre = spectrum[:patch_grid_height].reshape(patch_grid_height, modes, blocks, width)
    zim = spectrum[patch_grid_height:].reshape(patch_grid_height, modes, blocks, width)
    hre = jnp.tanh(block_product(zre, w_first[0]) - block_product(zim, w_first[1])).astype(
        jnp.bfloat16
    )
    him = jnp.tanh(block_product(zre, w_first[1]) + block_product(zim, w_first[0])).astype(
        jnp.bfloat16
    )
    spectrum_real = shrink(
        block_product(hre, w_second[0]) - block_product(him, w_second[1])
    ).astype(jnp.bfloat16)
    spectrum_imaginary = shrink(
        block_product(hre, w_second[1]) + block_product(him, w_second[0])
    ).astype(jnp.bfloat16)
    filtered = jnp.concatenate(
        [
            spectrum_real.reshape(patch_grid_height, modes, chans),
            spectrum_imaginary.reshape(patch_grid_height, modes, chans),
        ],
        axis=0,
    )
    inverse_transform = jnp.einsum(
        "qp,qmc->pmc", big_table, filtered, preferred_element_type=jnp.float32
    )
    inverse_transform = (inverse_transform * height_factors).astype(jnp.bfloat16)
    value_real = inverse_transform[:patch_grid_height]
    value_imaginary = inverse_transform[patch_grid_height:]
    part_re, part_im = (
        lax.all_to_all(value_real, "row", split_axis=0, concat_axis=1, tiled=True),
        lax.all_to_all(value_imaginary, "row", split_axis=0, concat_axis=1, tiled=True),
    )
    line_re, line_im = (
        lax.all_to_all(part_re, "col", split_axis=0, concat_axis=1, tiled=True),
        lax.all_to_all(part_im, "col", split_axis=0, concat_axis=1, tiled=True),
    )
    filter_coefficient = jnp.where(jnp.arange(half) == 0, 1.0, 2.0).astype(jnp.float32)
    inverse_w = jnp.concatenate(
        [
            (cos_w.astype(jnp.float32) * filter_coefficient).T,
            -(sin_w.astype(jnp.float32) * filter_coefficient).T,
        ],
        axis=0,
    ).astype(jnp.bfloat16)
    lines = jnp.concatenate([line_re, line_im], axis=1)
    spectral = jnp.einsum("hkc,kw->hwc", lines, inverse_w, preferred_element_type=jnp.float32)
    spectral = (spectral * width_factors).astype(jnp.bfloat16)
    home = lax.all_to_all(spectral, "col", split_axis=1, concat_axis=0, tiled=True)
    return (xf + home.astype(jnp.float32) + conv).astype(jnp.bfloat16)


def solution(mesh):
    return jax.shard_map(
        local,
        mesh=mesh,
        in_specs=(P("row", "col", None), P(), P(), P(), P()),
        out_specs=P("row", "col", None),
        check_vma=False,
    )
```

profile of v0, /device:TPU:0, one launch (start us, length us, event | category | flops | bytes accessed | tf_op | source)
XLA Modules:
  0.0 185.1 jit_solution(11169948337109951081)
XLA Ops:
  5.1 5.2 %all-to-all-start = ((bf16[32,64,256]{2,1,0:T(8,128)(2,1)}), bf16[32,64,256]{2,1,0:T(8,128)(2,1)S(1)}, u32[]{:S(2)}, u32[]{:S(2)}) async-start(bf16[32,64,256]{2,1,0:T(8,128)(2,1)} %fusion.4), calls=%async_computation | async-start | bytes 2097152 | tf_op jit(solution)/shard_map/all_to_all | solution.py:59
  11.3 12.6 %all-to-all-done = bf16[32,64,256]{2,1,0:T(8,128)(2,1)S(1)} async-done(((bf16[32,64,256]{2,1,0:T(8,128)(2,1)}), bf16[32,64,256]{2,1,0:T(8,128)(2,1)S(1)}, u32[]{:S(2)}, u32[]{:S(2)}) %all-to-all-start) | async-done | bytes 1048608 | tf_op jit(solution)/shard_map/all_to_all | solution.py:59
  25.7 3.5 %all-to-all-start.1 = ((bf16[8,128,256]{2,0,1:T(8,128)(2,1)}), bf16[8,128,256]{2,0,1:T(8,128)(2,1)S(1)}, u32[]{:S(2)}, u32[]{:S(2)}) async-start(bf16[8,128,256]{2,0,1:T(8,128)(2,1)} %copy.86), calls=%async_computation.1 | async-start | bytes 1048576 | tf_op jit(solution)/shard_map/all_to_all | solution.py:72
  30.3 6.4 %all-to-all-done.1 = bf16[8,128,256]{2,0,1:T(8,128)(2,1)S(1)} async-done(((bf16[8,128,256]{2,0,1:T(8,128)(2,1)}), bf16[8,128,256]{2,0,1:T(8,128)(2,1)S(1)}, u32[]{:S(2)}, u32[]{:S(2)}) %all-to-all-start.1) | async-done | bytes 524320 | tf_op jit(solution)/shard_map/all_to_all | solution.py:72
  36.6 3.5 %all-to-all-start.3 = ((bf16[8,128,256]{2,0,1:T(8,128)(2,1)}), bf16[8,128,256]{2,0,1:T(8,128)(2,1)S(1)}, u32[]{:S(2)}, u32[]{:S(2)}) async-start(bf16[8,128,256]{2,0,1:T(8,128)(2,1)} %copy.91), calls=%async_computation.3 | async-start | bytes 1048576 | tf_op jit(solution)/shard_map/all_to_all | solution.py:73
  41.3 5.4 %all-to-all-done.3 = bf16[8,128,256]{2,0,1:T(8,128)(2,1)S(1)} async-done(((bf16[8,128,256]{2,0,1:T(8,128)(2,1)}), bf16[8,128,256]{2,0,1:T(8,128)(2,1)S(1)}, u32[]{:S(2)}, u32[]{:S(2)}) %all-to-all-start.3) | async-done | bytes 524320 | tf_op jit(solution)/shard_map/all_to_all | solution.py:73
  46.7 4.9 %all-to-all-start.2 = ((bf16[32,32,256]{2,0,1:T(8,128)(2,1)}), bf16[32,32,256]{2,0,1:T(8,128)(2,1)S(1)}, u32[]{:S(2)}, u32[]{:S(2)}) async-start(bf16[32,32,256]{2,0,1:T(8,128)(2,1)} %copy.89), calls=%async_computation.2 | async-start | bytes 1048576 | tf_op jit(solution)/shard_map/all_to_all | solution.py:76
  52.8 14.2 %all-to-all-done.2 = bf16[32,32,256]{2,0,1:T(8,128)(2,1)S(1)} async-done(((bf16[32,32,256]{2,0,1:T(8,128)(2,1)}), bf16[32,32,256]{2,0,1:T(8,128)(2,1)S(1)}, u32[]{:S(2)}, u32[]{:S(2)}) %all-to-all-start.2) | async-done | bytes 524320 | tf_op jit(solution)/shard_map/all_to_all | solution.py:76
  67.0 3.5 %all-to-all-start.4 = ((bf16[32,32,256]{2,0,1:T(8,128)(2,1)}), bf16[32,32,256]{2,0,1:T(8,128)(2,1)S(1)}, u32[]{:S(2)}, u32[]{:S(2)}) async-start(bf16[32,32,256]{2,0,1:T(8,128)(2,1)} %copy.94), calls=%async_computation.4 | async-start | bytes 1048576 | tf_op jit(solution)/shard_map/all_to_all | solution.py:77
  72.9 12.9 %all-to-all-done.4 = bf16[32,32,256]{2,0,1:T(8,128)(2,1)S(1)} async-done(((bf16[32,32,256]{2,0,1:T(8,128)(2,1)}), bf16[32,32,256]{2,0,1:T(8,128)(2,1)S(1)}, u32[]{:S(2)}, u32[]{:S(2)}) %all-to-all-start.4) | async-done | bytes 524320 | tf_op jit(solution)/shard_map/all_to_all | solution.py:77
  94.8 3.5 %all-to-all-start.5 = ((bf16[256,4,256]{2,1,0:T(4,128)(2,1)}), bf16[256,4,256]{2,1,0:T(4,128)(2,1)S(1)}, u32[]{:S(2)}, u32[]{:S(2)}) async-start(bf16[256,4,256]{2,1,0:T(4,128)(2,1)} %copy.112), calls=%async_computation.5 | async-start | bytes 1048576 | tf_op jit(solution)/shard_map/all_to_all | solution.py:115
  99.3 14.2 %all-to-all-done.5 = bf16[256,4,256]{2,1,0:T(4,128)(2,1)S(1)} async-done(((bf16[256,4,256]{2,1,0:T(4,128)(2,1)}), bf16[256,4,256]{2,1,0:T(4,128)(2,1)S(1)}, u32[]{:S(2)}, u32[]{:S(2)}) %all-to-all-start.5) | async-done | bytes 524320 | tf_op jit(solution)/shard_map/all_to_all | solution.py:115
  113.6 3.7 %all-to-all-start.7 = ((bf16[256,4,256]{2,1,0:T(4,128)(2,1)}), bf16[256,4,256]{2,1,0:T(4,128)(2,1)S(1)}, u32[]{:S(2)}, u32[]{:S(2)}) async-start(bf16[256,4,256]{2,1,0:T(4,128)(2,1)} %copy.117), calls=%async_computation.7 | async-start | bytes 1048576 | tf_op jit(solution)/shard_map/all_to_all | solution.py:116
  118.5 14.0 %all-to-all-done.7 = bf16[256,4,256]{2,1,0:T(4,128)(2,1)S(1)} async-done(((bf16[256,4,256]{2,1,0:T(4,128)(2,1)}), bf16[256,4,256]{2,1,0:T(4,128)(2,1)S(1)}, u32[]{:S(2)}, u32[]{:S(2)}) %all-to-all-start.7) | async-done | bytes 524320 | tf_op jit(solution)/shard_map/all_to_all | solution.py:116
  132.5 3.5 %all-to-all-start.6 = ((bf16[32,32,256]{2,1,0:T(8,128)(2,1)}), bf16[32,32,256]{2,1,0:T(8,128)(2,1)S(1)}, u32[]{:S(2)}, u32[]{:S(2)}) async-start(bf16[32,32,256]{2,1,0:T(8,128)(2,1)} %copy.115), calls=%async_computation.6 | async-start | bytes 1048576 | tf_op jit(solution)/shard_map/all_to_all | solution.py:119
  137.2 6.9 %all-to-all-done.6 = bf16[32,32,256]{2,1,0:T(8,128)(2,1)S(1)} async-done(((bf16[32,32,256]{2,1,0:T(8,128)(2,1)}), bf16[32,32,256]{2,1,0:T(8,128)(2,1)S(1)}, u32[]{:S(2)}, u32[]{:S(2)}) %all-to-all-start.6) | async-done | bytes 524320 | tf_op jit(solution)/shard_map/all_to_all | solution.py:119
  144.1 3.5 %all-to-all-start.8 = ((bf16[32,32,256]{2,1,0:T(8,128)(2,1)}), bf16[32,32,256]{2,1,0:T(8,128)(2,1)S(1)}, u32[]{:S(2)}, u32[]{:S(2)}) async-start(bf16[32,32,256]{2,1,0:T(8,128)(2,1)} %copy.120), calls=%async_computation.8 | async-start | bytes 1048576 | tf_op jit(solution)/shard_map/all_to_all | solution.py:120
  148.2 6.6 %all-to-all-done.8 = bf16[32,32,256]{2,1,0:T(8,128)(2,1)S(1)} async-done(((bf16[32,32,256]{2,1,0:T(8,128)(2,1)}), bf16[32,32,256]{2,1,0:T(8,128)(2,1)S(1)}, u32[]{:S(2)}, u32[]{:S(2)}) %all-to-all-start.8) | async-done | bytes 524320 | tf_op jit(solution)/shard_map/all_to_all | solution.py:120
  156.8 4.4 %all-to-all-start.9 = ((bf16[8,256,256]{2,0,1:T(8,128)(2,1)}), bf16[8,256,256]{2,0,1:T(8,128)(2,1)}, u32[]{:S(2)}, u32[]{:S(2)}) async-start(bf16[8,256,256]{2,0,1:T(8,128)(2,1)} %copy.122), calls=%async_computation.9 | async-start | bytes 2097152 | tf_op jit(solution)/shard_map/all_to_all | solution.py:133
  162.0 3.5 %collective-permute-start.1 = (bf16[1,64,256]{2,1,0:T(8,128)(2,1)S(1)}, bf16[1,64,256]{2,1,0:T(8,128)(2,1)S(1)}, u32[]{:S(2)}, u32[]{:S(2)}) collective-permute-start(bf16[1,64,256]{2,1,0:T(8,128)(2,1)S(1)} %get-tuple-element.10), channel_id=1, source_target_pairs={{4,0},{8,4},{12,8},{16,12},{20,16},{24,20},{28,24},{0,28},{5,1},{9... | collective-permute-start | bytes 98312 | tf_op jit(solution)/shard_map/ppermute | solution.py:17
  168.2 2.0 %collective-permute-start.2 = (bf16[34,1,256]{2,1,0:T(2,128)(2,1)S(1)}, bf16[34,1,256]{2,1,0:T(2,128)(2,1)S(1)}, u32[]{:S(2)}, u32[]{:S(2)}) collective-permute-start(bf16[34,1,256]{2,1,0:T(2,128)(2,1)S(1)} %get-tuple-element.7), channel_id=1, source_target_pairs={{0,1},{1,2},{2,3},{3,0},{4,5},{5,6},{6,7},{7,4},{8,9},{9,10},{10,1... | collective-permute-start | bytes 52232 | tf_op jit(solution)/shard_map/ppermute | solution.py:16
  171.8 3.4 %collective-permute-done.2 = bf16[34,1,256]{2,1,0:T(2,128)(2,1)S(1)} collective-permute-done((bf16[34,1,256]{2,1,0:T(2,128)(2,1)S(1)}, bf16[34,1,256]{2,1,0:T(2,128)(2,1)S(1)}, u32[]{:S(2)}, u32[]{:S(2)}) %collective-permute-start.2) | collective-permute-done | bytes 17440 | tf_op jit(solution)/shard_map/ppermute | solution.py:16
  175.2 2.4 %maximum_maximum_fusion = (bf16[34,65,256]{2,1,0:T(8,128)(2,1)S(1)}, bf16[34,65,256]{2,1,0:T(8,128)(2,1)S(1)}) fusion(bf16[1,64,256]{2,1,0:T(8,128)(2,1)S(1)} %collective-permute-done.1, bf16[32,64,256]{2,1,0:T(8,128)(2,1)} %fusion.4, bf16[1,64,256]{2,1,0:T(8,128)(2,1)S(1)} %collective-permute-done, bf16[34,1,256]{2,1,0:T(2,128)(2,1)S(1)} %collective-permute-done.2, ...), kind=kLoop, calls=%fused_computation.25 | loop fusion | flops 9052160 | bytes 3411968 | tf_op jit(solution)/shard_map/concatenate | solution.py:18
  179.8 5.2 %fusion.6 = bf16[32,64,256]{2,1,0:T(8,128)(2,1)} fusion(bf16[32,64,256]{2,1,0:T(8,128)(2,1)S(1)} %copy-done, f32[4,8,64,256]{3,2,1,0:T(8,128)S(1)} %copy.123, bf16[32,64,256]{2,1,0:T(8,128)(2,1)} %fusion.4, bf16[34,65,256]{2,1,0:T(8,128)(2,1)S(1)} %get-tuple-element.6, bf16[1,64,256]{2,1,0:T(8,128)(2,1)S(1)} %copy-done.6, ...), kind=kLoop, calls=%fused_computation.9 | loop fusion | flops 16777216 | bytes 11609088 | tf_op jit(solution)/shard_map/convert_element_type | solution.py:134
  (105 shorter events, 35.8 us)
Async XLA Ops:
  0.0 3.6 %copy-start = (bf16[32,64,256]{2,1,0:T(8,128)(2,1)S(1)}, bf16[32,64,256]{2,1,0:T(8,128)(2,1)}, u32[]{:S(2)}) copy-start(bf16[32,64,256]{2,1,0:T(8,128)(2,1)} %param.5) | copy-start | bytes 3145732
  0.0 3.6 %copy-start.20 = (f32[256]{0:T(256)S(1)}, f32[256]{0:T(256)}, u32[]{:S(2)}) copy-start(f32[256]{0:T(256)} %param.6) | copy-start | bytes 3076
  5.1 18.8 %all-to-all-start = ((bf16[32,64,256]{2,1,0:T(8,128)(2,1)}), bf16[32,64,256]{2,1,0:T(8,128)(2,1)S(1)}, u32[]{:S(2)}, u32[]{:S(2)}) async-start(bf16[32,64,256]{2,1,0:T(8,128)(2,1)} %fusion.4), calls=%async_computation | async-start | bytes 2097152 | tf_op jit(solution)/shard_map/all_to_all | solution.py:59
  25.7 10.9 %all-to-all-start.1 = ((bf16[8,128,256]{2,0,1:T(8,128)(2,1)}), bf16[8,128,256]{2,0,1:T(8,128)(2,1)S(1)}, u32[]{:S(2)}, u32[]{:S(2)}) async-start(bf16[8,128,256]{2,0,1:T(8,128)(2,1)} %copy.86), calls=%async_computation.1 | async-start | bytes 1048576 | tf_op jit(solution)/shard_map/all_to_all | solution.py:72
  36.6 10.1 %all-to-all-start.3 = ((bf16[8,128,256]{2,0,1:T(8,128)(2,1)}), bf16[8,128,256]{2,0,1:T(8,128)(2,1)S(1)}, u32[]{:S(2)}, u32[]{:S(2)}) async-start(bf16[8,128,256]{2,0,1:T(8,128)(2,1)} %copy.91), calls=%async_computation.3 | async-start | bytes 1048576 | tf_op jit(solution)/shard_map/all_to_all | solution.py:73
  46.7 20.3 %all-to-all-start.2 = ((bf16[32,32,256]{2,0,1:T(8,128)(2,1)}), bf16[32,32,256]{2,0,1:T(8,128)(2,1)S(1)}, u32[]{:S(2)}, u32[]{:S(2)}) async-start(bf16[32,32,256]{2,0,1:T(8,128)(2,1)} %copy.89), calls=%async_computation.2 | async-start | bytes 1048576 | tf_op jit(solution)/shard_map/all_to_all | solution.py:76
  67.0 18.8 %all-to-all-start.4 = ((bf16[32,32,256]{2,0,1:T(8,128)(2,1)}), bf16[32,32,256]{2,0,1:T(8,128)(2,1)S(1)}, u32[]{:S(2)}, u32[]{:S(2)}) async-start(bf16[32,32,256]{2,0,1:T(8,128)(2,1)} %copy.94), calls=%async_computation.4 | async-start | bytes 1048576 | tf_op jit(solution)/shard_map/all_to_all | solution.py:77
  72.6 13.4 %copy-start.8 = (bf16[256,256]{1,0:T(8,128)(2,1)}, bf16[256,256]{1,0:T(8,128)(2,1)S(1)}, u32[]{:S(2)}) copy-start(bf16[256,256]{1,0:T(8,128)(2,1)S(1)} %get-tuple-element.29) | copy-start | bytes 393220
  86.8 0.9 copy-start.1
  88.0 0.9 copy-start.7
  90.0 0.8 copy-start.2
  91.0 1.8 copy-start.9
  94.8 18.8 %all-to-all-start.5 = ((bf16[256,4,256]{2,1,0:T(4,128)(2,1)}), bf16[256,4,256]{2,1,0:T(4,128)(2,1)S(1)}, u32[]{:S(2)}, u32[]{:S(2)}) async-start(bf16[256,4,256]{2,1,0:T(4,128)(2,1)} %copy.112), calls=%async_computation.5 | async-start | bytes 1048576 | tf_op jit(solution)/shard_map/all_to_all | solution.py:115
  113.6 19.0 %all-to-all-start.7 = ((bf16[256,4,256]{2,1,0:T(4,128)(2,1)}), bf16[256,4,256]{2,1,0:T(4,128)(2,1)S(1)}, u32[]{:S(2)}, u32[]{:S(2)}) async-start(bf16[256,4,256]{2,1,0:T(4,128)(2,1)} %copy.117), calls=%async_computation.7 | async-start | bytes 1048576 | tf_op jit(solution)/shard_map/all_to_all | solution.py:116
  132.5 11.5 %all-to-all-start.6 = ((bf16[32,32,256]{2,1,0:T(8,128)(2,1)}), bf16[32,32,256]{2,1,0:T(8,128)(2,1)S(1)}, u32[]{:S(2)}, u32[]{:S(2)}) async-start(bf16[32,32,256]{2,1,0:T(8,128)(2,1)} %copy.115), calls=%async_computation.6 | async-start | bytes 1048576 | tf_op jit(solution)/shard_map/all_to_all | solution.py:119
  144.1 10.7 %all-to-all-start.8 = ((bf16[32,32,256]{2,1,0:T(8,128)(2,1)}), bf16[32,32,256]{2,1,0:T(8,128)(2,1)S(1)}, u32[]{:S(2)}, u32[]{:S(2)}) async-start(bf16[32,32,256]{2,1,0:T(8,128)(2,1)} %copy.120), calls=%async_computation.8 | async-start | bytes 1048576 | tf_op jit(solution)/shard_map/all_to_all | solution.py:120
  156.8 14.4 %copy-start.10 = (f32[3,3,256]{2,1,0:T(4,128)S(1)}, f32[3,3,256]{2,1,0:T(4,128)}, u32[]{:S(2)}) copy-start(f32[3,3,256]{2,1,0:T(4,128)} %param.9) | copy-start | bytes 27652
  156.8 20.7 %all-to-all-start.9 = ((bf16[8,256,256]{2,0,1:T(8,128)(2,1)}), bf16[8,256,256]{2,0,1:T(8,128)(2,1)}, u32[]{:S(2)}, u32[]{:S(2)}) async-start(bf16[8,256,256]{2,0,1:T(8,128)(2,1)} %copy.122), calls=%async_computation.9 | async-start | bytes 2097152 | tf_op jit(solution)/shard_map/all_to_all | solution.py:133
  162.0 5.1 %collective-permute-start = (bf16[1,64,256]{2,1,0:T(8,128)(2,1)S(1)}, bf16[1,64,256]{2,1,0:T(8,128)(2,1)S(1)}, u32[]{:S(2)}, u32[]{:S(2)}) collective-permute-start(bf16[1,64,256]{2,1,0:T(8,128)(2,1)S(1)} %get-tuple-element.9), channel_id=1, source_target_pairs={{0,4},{4,8},{8,12},{12,16},{16,20},{20,24},{24,28},{28,0},{1,5},{5... | collective-permute-start | bytes 98312 | tf_op jit(solution)/shard_map/ppermute | solution.py:16
  162.0 5.1 %collective-permute-start.1 = (bf16[1,64,256]{2,1,0:T(8,128)(2,1)S(1)}, bf16[1,64,256]{2,1,0:T(8,128)(2,1)S(1)}, u32[]{:S(2)}, u32[]{:S(2)}) collective-permute-start(bf16[1,64,256]{2,1,0:T(8,128)(2,1)S(1)} %get-tuple-element.10), channel_id=1, source_target_pairs={{4,0},{8,4},{12,8},{16,12},{20,16},{24,20},{28,24},{0,28},{5,1},{9... | collective-permute-start | bytes 98312 | tf_op jit(solution)/shard_map/ppermute | solution.py:17
  167.1 8.0 %copy-start.3 = (bf16[1,64,256]{2,1,0:T(8,128)(2,1)}, bf16[1,64,256]{2,1,0:T(8,128)(2,1)S(1)}, u32[]{:S(2)}) copy-start(bf16[1,64,256]{2,1,0:T(8,128)(2,1)S(1)} %collective-permute-done) | copy-start | bytes 98308
  167.1 8.0 %copy-start.5 = (bf16[1,64,256]{2,1,0:T(8,128)(2,1)}, bf16[1,64,256]{2,1,0:T(8,128)(2,1)S(1)}, u32[]{:S(2)}) copy-start(bf16[1,64,256]{2,1,0:T(8,128)(2,1)S(1)} %collective-permute-done.1) | copy-start | bytes 98308
  168.2 7.0 %collective-permute-start.2 = (bf16[34,1,256]{2,1,0:T(2,128)(2,1)S(1)}, bf16[34,1,256]{2,1,0:T(2,128)(2,1)S(1)}, u32[]{:S(2)}, u32[]{:S(2)}) collective-permute-start(bf16[34,1,256]{2,1,0:T(2,128)(2,1)S(1)} %get-tuple-element.7), channel_id=1, source_target_pairs={{0,1},{1,2},{2,3},{3,0},{4,5},{5,6},{6,7},{7,4},{8,9},{9,10},{10,1... | collective-permute-start | bytes 52232 | tf_op jit(solution)/shard_map/ppermute | solution.py:16
  170.2 5.0 %collective-permute-start.3 = (bf16[34,1,256]{2,1,0:T(2,128)(2,1)S(1)}, bf16[34,1,256]{2,1,0:T(2,128)(2,1)S(1)}, u32[]{:S(2)}, u32[]{:S(2)}) collective-permute-start(bf16[34,1,256]{2,1,0:T(2,128)(2,1)S(1)} %get-tuple-element.8), channel_id=1, source_target_pairs={{1,0},{2,1},{3,2},{0,3},{5,4},{6,5},{7,6},{4,7},{9,8},{10,9},{11,1... | collective-permute-start | bytes 52232 | tf_op jit(solution)/shard_map/ppermute | solution.py:17
  (11 other events, 8.4 us)
where the time goes:
time: 186 us; the launch traced here: 185 us
  waiting for transfers between devices  98.1 us (53%)
  starting transfers between devices  45.6 us (25%)
  other arithmetic  18.8 us (10%)
  local copies, waits for them, and re-layouts  15.5 us (8%)
  matrix products  6.54 us (4%)
    all_to_all x1, waiting for transfers between devices, local(): lax.all_to_all(value_real, 'row', split_axis=0, concat_axis=1, tiled=True)  14.2 us
    all_to_all x1, waiting for transfers between devices, local(): lax.all_to_all(across_re, 'row', split_axis=1, concat_axis=0, tiled=True)  14.2 us
    all_to_all x1, waiting for transfers between devices, local(): lax.all_to_all(value_imaginary, 'row', split_axis=0, concat_axis=1, tiled...  14 us
    all_to_all x1, waiting for transfers between devices, local(): lax.all_to_all(across_im, 'row', split_axis=1, concat_axis=0, tiled=True)  12.9 us
    all_to_all x1, waiting for transfers between devices, local(): lax.all_to_all(normed, 'col', split_axis=0, concat_axis=1, tiled=True)  12.6 us
    all_to_all x1, waiting for transfers between devices, local(): lax.all_to_all(part_re, 'col', split_axis=0, concat_axis=1, tiled=True)  6.86 us
    convert_element_type x2, other arithmetic, local(): return (xf + home.astype(jnp.float32) + conv).astype(jnp.bfloat16)  6.61 us
    all_to_all x1, waiting for transfers between devices, local(): lax.all_to_all(part_im, 'col', split_axis=0, concat_axis=1, tiled=True)  6.6 us
  transfers between devices with their start and end apart: 14, of which 11 were waited for; matrix products, arithmetic and copies ran while one was open for 9% of the time, Pallas kernels for 0%

commit v1 on v0

--- a/solution.py
+++ b/solution.py
@@ -1,8 +1,13 @@
+import functools
 import math
 
 import jax
 import jax.numpy as jnp
+import ml_dtypes
+import numpy as np
 from jax import lax
+from jax.experimental import pallas as pl
+from jax.experimental.pallas import tpu as pltpu
 from jax.sharding import PartitionSpec as P
 
 
@@ -36,7 +41,7 @@
     return jnp.einsum("qmbc,bcd->qmbd", left, weight, preferred_element_type=jnp.float32)
 
 
-def local(patches, norm_gain, w_first, w_second, depth_kernel):
+def general(patches, norm_gain, w_first, w_second, depth_kernel):
     n_row = lax.axis_size("row")
     n_col = lax.axis_size("col")
     rows_dev, cols_dev, chans = patches.shape
@@ -134,6 +139,480 @@
     return (xf + home.astype(jnp.float32) + conv).astype(jnp.bfloat16)
 
 
+LANES = 128
+PAIR = 64
+TILE = 16
+COL_CHUNKS = 4
+KGROUPS = 2
+
+
+def row_order(n_row, rows_dev):
+    pairs = rows_dev // 2
+    zc = rows_dev // TILE
+    per = pairs // zc
+    order = []
+    for z in range(zc):
+        for s in range(n_row):
+            for slot in range(TILE):
+                order.append(s * rows_dev + (slot // per) * pairs + z * per + slot % per)
+    return np.array(order)
+
+
+def host_tables(grid_h, grid_w, n_row, rows_dev):
+    half = grid_w // 2
+
+    def table(a, b, n):
+        phase = (np.outer(a, b) % n).astype(np.float32) * np.float32(2.0 * math.pi / n)
+        bf16 = ml_dtypes.bfloat16
+        cos, sin = (np.cos(phase).astype(bf16), np.sin(phase).astype(bf16))
+        return cos.astype(np.float32), sin.astype(np.float32)
+
+    cos_w, sin_w = table(np.arange(half), np.arange(grid_w), grid_w)
+    weight = np.where(np.arange(half) == 0, 1.0, 2.0).astype(np.float32)[:, None]
+    forward = np.concatenate([cos_w, -sin_w], axis=0)
+    inverse = np.concatenate([cos_w * weight, -sin_w * weight], axis=0).T
+    order = row_order(n_row, rows_dev)
+    cos_h, sin_h = table(order, order, grid_h)
+    swap = np.zeros((TILE, TILE, TILE, TILE), np.float32)
+    for a in range(TILE):
+        for b in range(TILE):
+            swap[a, b, b, a] = 1.0
+    cast = lambda v: v.astype(ml_dtypes.bfloat16)
+    return (
+        cast(forward),
+        cast(inverse),
+        cast(np.concatenate([cos_h, sin_h], axis=0)),
+        cast(swap.reshape(TILE * TILE, TILE * TILE)),
+    )
+
+
+def half_turn(x):
+    return pltpu.roll(x, PAIR, x.ndim - 1)
+
+
+def low_lanes(shape):
+    return lax.broadcasted_iota(jnp.int32, shape, len(shape) - 1) < PAIR
+
+
+def swap_halves(a, b):
+    low = low_lanes(a.shape)
+    return jnp.where(low, a, half_turn(b)), jnp.where(low, half_turn(a), b)
+
+
+def mixing_kernel(
+    n_row,
+    n_col,
+    scale_w,
+    scale_h,
+    patches,
+    gain,
+    w_first,
+    w_second,
+    depth,
+    forward_ref,
+    inverse_ref,
+    height_ref,
+    swap_ref,
+    out,
+    send1,
+    recv1,
+    turned,
+    send2,
+    recv2,
+    send3,
+    recv3,
+    send4,
+    recv4,
+    conv,
+    rim_send,
+    rim_recv,
+    rim,
+    s1,
+    r1,
+    s2,
+    r2,
+    s3,
+    r3,
+    s4,
+    r4,
+    sh,
+    rh,
+):
+    f32, bf16 = jnp.float32, jnp.bfloat16
+    row, col = lax.axis_index("row"), lax.axis_index("col")
+    rows_dev, cols_dev, chans = patches.shape
+    pairs = rows_dev // 2
+    per_col = pairs // COL_CHUNKS
+    zc = rows_dev // TILE
+    per_z = pairs // zc
+    col_per_z = COL_CHUNKS // zc
+    grid_w = cols_dev * n_col
+    half = grid_w // 2
+    kl = half // n_row
+    per_k = kl // KGROUPS
+    groups = chans // LANES
+
+    def col_peer(d):
+        return lax.rem(col + d, n_col)
+
+    def row_peer(d):
+        return lax.rem(row + d, n_row)
+
+    def to_col(d):
+        return {"col": col_peer(d)}
+
+    def to_row(d):
+        return {"row": row_peer(d)}
+
+    def dot(a, b):
+        return jnp.dot(a, b, preferred_element_type=f32)
+
+    barrier = pltpu.get_barrier_semaphore()
+    for d in range(1, n_col):
+        pl.semaphore_signal(barrier, inc=1, device_id=to_col(d), device_id_type=pl.DeviceIdType.MESH)
+    for d in range(1, n_row):
+        pl.semaphore_signal(barrier, inc=1, device_id=to_row(d), device_id_type=pl.DeviceIdType.MESH)
+
+    def copy1(ch, d):
+        return pltpu.make_async_remote_copy(
+            src_ref=send1.at[ch, col_peer(d)],
+            dst_ref=recv1.at[ch, col],
+            send_sem=s1.at[ch, d - 1],
+            recv_sem=r1.at[ch, d - 1],
+            device_id=to_col(d),
+            device_id_type=pl.DeviceIdType.MESH,
+        )
+
+    def copy2(z, g, d):
+        ks = pl.ds(g * per_k, per_k)
+        return pltpu.make_async_remote_copy(
+            src_ref=send2.at[z, row_peer(d), ks],
+            dst_ref=recv2.at[z, row, ks],
+            send_sem=s2.at[z, g, d - 1],
+            recv_sem=r2.at[z, g, d - 1],
+            device_id=to_row(d),
+            device_id_type=pl.DeviceIdType.MESH,
+        )
+
+    def copy3(z, g, d):
+        ks = pl.ds(g * per_k, per_k)
+        return pltpu.make_async_remote_copy(
+            src_ref=send3.at[z, row_peer(d), ks],
+            dst_ref=recv3.at[z, row, ks],
+            send_sem=s3.at[z, g, d - 1],
+            recv_sem=r3.at[z, g, d - 1],
+            device_id=to_row(d),
+            device_id_type=pl.DeviceIdType.MESH,
+        )
+
+    def copy4(ch, d):
+        return pltpu.make_async_remote_copy(
+            src_ref=send4.at[ch, col_peer(d)],
+            dst_ref=recv4.at[ch, col],
+            send_sem=s4.at[ch, d - 1],
+            recv_sem=r4.at[ch, d - 1],
+            device_id=to_col(d),
+            device_id_type=pl.DeviceIdType.MESH,
+        )
+
+    def copy_rim(side):
+        return pltpu.make_async_remote_copy(
+            src_ref=rim_send.at[side],
+            dst_ref=rim_recv.at[side],
+            send_sem=sh.at[side],
+            recv_sem=rh.at[side],
+            device_id=to_row(1 if side == 0 else n_row - 1),
+            device_id_type=pl.DeviceIdType.MESH,
+        )
+
+    def normed_row(h):
+        x = patches[h].astype(f32)
+        mean = jnp.mean(x, axis=-1, keepdims=True)
+        centred = x - mean
+        var = jnp.mean(centred * centred, axis=-1, keepdims=True)
+        return centred * lax.rsqrt(var + 1e-05) * gain[...]
+
+    for ch in range(COL_CHUNKS):
+
+        def norm_pair(i, carry, ch=ch):
+            hp = ch * per_col + i
+            lower, upper = normed_row(hp), normed_row(hp + pairs)
+            for j in range(groups):
+                lanes = slice(j * LANES, (j + 1) * LANES)
+                even, odd = swap_halves(lower[:, lanes], upper[:, lanes])
+                send1[ch, 2 * j, i] = even.astype(bf16)
+                send1[ch, 2 * j + 1, i] = odd.astype(bf16)
+            return carry
+
+        lax.fori_loop(0, per_col, norm_pair, 0)
+        if ch == 0:
+            pl.semaphore_wait(barrier, n_col + n_row - 2)
+        for d in range(1, n_col):
+            copy1(ch, d).start()
+        recv1[ch, col] = send1[ch, col]
+
+    def line(ch, i):
+        return recv1[ch, :, i].reshape(grid_w, LANES)
+
+    for z in range(zc):
+        for ch in range(z * col_per_z, (z + 1) * col_per_z):
+            for d in range(1, n_col):
+                copy1(ch, d).wait_recv()
+
+            def width_pair(i, carry, ch=ch, z=z):
+                y = dot(forward_ref[...], line(ch, i)) * scale_w
+                lower, upper = swap_halves(y[:half], y[half:])
+                slot = (ch - z * col_per_z) * per_col + i
+                turned[slot] = lower.astype(bf16)
+                turned[per_z + slot] = upper.astype(bf16)
+                return carry
+
+            lax.fori_loop(0, per_col, width_pair, 0)
+
+        def turn_out(r, carry, z=z):
+            ks = pl.ds(pl.multiple_of(r * kl, kl), kl)
+            tile = turned[:, ks, :].reshape(TILE * kl, LANES)
+            send2[z, r] = dot(swap_ref[...], tile).astype(bf16).reshape(kl, TILE, LANES)
+            return carry
+
+        lax.fori_loop(0, n_row, turn_out, 0)
+        for g in range(KGROUPS):
+            for d in range(1, n_row):
+                copy2(z, g, d).start()
+        recv2[z, row] = send2[z, row]
+
+    first = line(0, 0).astype(f32)
+    final = line(COL_CHUNKS - 1, per_col - 1).astype(f32)
+    rim_send[0] = swap_halves(final[:half], final[half:])[1].astype(bf16)
+    rim_send[1] = swap_halves(first[:half], first[half:])[0].astype(bf16)
+    for side in range(2):
+        copy_rim(side).start()
+
+    def complex_weight(ref):
+        re, im = ref[0, col].astype(f32), ref[1, col].astype(f32)
+        return jnp.concatenate(
+            [jnp.concatenate([re, im], axis=1), jnp.concatenate([-im, re], axis=1)], axis=0
+        ).astype(bf16)
+
+    weight_a, weight_b = complex_weight(w_first), complex_weight(w_second)
+
+    lane_group = pl.multiple_of((col // 2) * LANES, LANES)
+    own = depth[:, pl.ds(lane_group, LANES)]
+    low = low_lanes(own.shape)
+    other = half_turn(own)
+    taps = jnp.where((col % 2) == 0, jnp.where(low, own, other), jnp.where(low, other, own))
+    for side in range(2):
+        copy_rim(side).wait_recv()
+    before = rim_recv[0].astype(f32)
+    after = rim_recv[1].astype(f32)
+    before = jnp.concatenate([before, half_turn(before)], axis=0)
+    after = jnp.concatenate([half_turn(after), after], axis=0)
+    low = low_lanes(before.shape)
+    rim[0] = jnp.where(low, before, half_turn(final)).astype(bf16)
+    rim[1] = jnp.where(low, half_turn(first), after).astype(bf16)
+
+    def conv_pair(hp, above, here, below):
+        total = None
+        for j in range(3):
+            part = None
+            for i, rows in enumerate((above, here, below)):
+                term = rows * taps[3 * i + j : 3 * i + j + 1]
+                part = term if part is None else part + term
+            if j == 0:
+                part = pltpu.roll(part, 1, 0)
+            if j == 2:
+                part = pltpu.roll(part, grid_w - 1, 0)
+            total = part if total is None else total + part
+        conv[hp] = total
+
+    def at(hp):
+        return line(hp // per_col, hp % per_col).astype(f32)
+
+    conv_pair(0, rim[0].astype(f32), at(0), at(1))
+
+    def conv_inner(hp, carry):
+        conv_pair(hp, at(hp - 1), at(hp), at(hp + 1))
+        return carry
+
+    lax.fori_loop(1, pairs - 1, conv_inner, 0)
+    conv_pair(pairs - 1, at(pairs - 2), at(pairs - 1), rim[1].astype(f32))
+
+    def height(u):
+        both = dot(height_ref[...], u)
+        n = both.shape[0] // 2
+        turned_part = half_turn(both[n:])
+        return both[:n], jnp.where(low_lanes(turned_part.shape), turned_part, -turned_part)
+
+    grid_h = rows_dev * n_row
+
+    def filter_mode(k, carry):
+        u = recv2[:, :, k].reshape(grid_h, LANES)
+        a, b = height(u)
+        zed = ((a + b) * scale_h).astype(bf16)
+        hidden = jnp.tanh(dot(zed, weight_a)).astype(bf16)
+        s = dot(hidden, weight_b)
+        s = (s - jnp.clip(s, -0.25, 0.25)).astype(bf16)
+        a, b = height(s)
+        v = ((a - b) * scale_h).astype(bf16)
+        send3[:, :, k] = v.reshape(zc, n_row, TILE, LANES)
+        return carry
+
+    for g in range(KGROUPS):
+        for z in range(zc):
+            for d in range(1, n_row):
+                copy2(z, g, d).wait_recv()
+        lax.fori_loop(g * per_k, (g + 1) * per_k, filter_mode, 0)
+        for d in range(1, n_row):
+            copy3(0, g, d).start()
+    for z in range(1, zc):
+        for g in range(KGROUPS):
+            for d in range(1, n_row):
+                copy3(z, g, d).start()
+    for z in range(zc):
+        recv3[z, row] = send3[z, row]
+
+    for z in range(zc):
+        for g in range(KGROUPS):
+            for d in range(1, n_row):
+                copy3(z, g, d).wait_recv()
+
+        def turn_back(r, carry, z=z):
+            tile = recv3[z, r].reshape(kl * TILE, LANES)
+            ks = pl.ds(pl.multiple_of(r * kl, kl), kl)
+            turned[:, ks, :] = dot(swap_ref[...], tile).astype(bf16).reshape(TILE, kl, LANES)
+            return carry
+
+        lax.fori_loop(0, n_row, turn_back, 0)
+        for ch in range(z * col_per_z, (z + 1) * col_per_z):
+
+            def inverse_pair(i, carry, ch=ch, z=z):
+                slot = (ch - z * col_per_z) * per_col + i
+                re, im = swap_halves(turned[slot].astype(f32), turned[per_z + slot].astype(f32))
+                x = jnp.concatenate([re.astype(bf16), im.astype(bf16)], axis=0)
+                cells = dot(inverse_ref[...], x) * scale_w + conv[ch * per_col + i]
+                send4[ch, :, i] = cells.astype(bf16).reshape(n_col, cols_dev, LANES)
+                return carry
+
+            lax.fori_loop(0, per_col, inverse_pair, 0)
+            for d in range(1, n_col):
+                copy4(ch, d).start()
+            recv4[ch, col] = send4[ch, col]
+
+    for ch in range(COL_CHUNKS):
+        for d in range(1, n_col):
+            copy4(ch, d).wait_recv()
+
+        def finish_pair(i, carry, ch=ch):
+            hp = ch * per_col + i
+            for j in range(groups):
+                lanes = slice(j * LANES, (j + 1) * LANES)
+                lower, upper = swap_halves(
+                    recv4[ch, 2 * j, i].astype(f32), recv4[ch, 2 * j + 1, i].astype(f32)
+                )
+                out[hp, :, lanes] = (patches[hp, :, lanes].astype(f32) + lower).astype(bf16)
+                out[hp + pairs, :, lanes] = (
+                    patches[hp + pairs, :, lanes].astype(f32) + upper
+                ).astype(bf16)
+            return carry
+
+        lax.fori_loop(0, per_col, finish_pair, 0)
+
+    for ch in range(COL_CHUNKS):
+        for d in range(1, n_col):
+            copy1(ch, d).wait_send()
+            copy4(ch, d).wait_send()
+    for z in range(zc):
+        for g in range(KGROUPS):
+            for d in range(1, n_row):
+                copy2(z, g, d).wait_send()
+                copy3(z, g, d).wait_send()
+    for side in range(2):
+        copy_rim(side).wait_send()
+
+
+def fused(patches, norm_gain, w_first, w_second, depth_kernel):
+    n_row = lax.axis_size("row")
+    n_col = lax.axis_size("col")
+    rows_dev, cols_dev, chans = patches.shape
+    grid_h, grid_w = rows_dev * n_row, cols_dev * n_col
+    pairs, zc = rows_dev // 2, rows_dev // TILE
+    per_col = pairs // COL_CHUNKS
+    half = grid_w // 2
+    kl = half // n_row
+    tables = host_tables(grid_h, grid_w, n_row, rows_dev)
+    bf16, f32 = jnp.bfloat16, jnp.float32
+    vmem = pl.BlockSpec(memory_space=pltpu.VMEM)
+    col_buffer = pltpu.VMEM((COL_CHUNKS, n_col, per_col, cols_dev, LANES), bf16)
+    row_buffer = pltpu.VMEM((zc, n_row, kl, TILE, LANES), bf16)
+    col_sems = pltpu.SemaphoreType.DMA((COL_CHUNKS, n_col - 1))
+    row_sems = pltpu.SemaphoreType.DMA((zc, KGROUPS, n_row - 1))
+    rim_sems = pltpu.SemaphoreType.DMA((2,))
+    return pl.pallas_call(
+        functools.partial(
+            mixing_kernel, n_row, n_col, 1.0 / math.sqrt(grid_w), 1.0 / math.sqrt(grid_h)
+        ),
+        out_shape=jax.ShapeDtypeStruct(patches.shape, bf16),
+        in_specs=[vmem] * 9,
+        out_specs=vmem,
+        scratch_shapes=[
+            col_buffer,
+            col_buffer,
+            pltpu.VMEM((TILE, half, LANES), bf16),
+            row_buffer,
+            row_buffer,
+            row_buffer,
+            row_buffer,
+            col_buffer,
+            col_buffer,
+            pltpu.VMEM((pairs, grid_w, LANES), f32),
+            pltpu.VMEM((2, half, LANES), bf16),
+            pltpu.VMEM((2, half, LANES), bf16),
+            pltpu.VMEM((2, grid_w, LANES), bf16),
+            col_sems,
+            col_sems,
+            row_sems,
+            row_sems,
+            row_sems,
+            row_sems,
+            col_sems,
+            col_sems,
+            rim_sems,
+            rim_sems,
+        ],
+        compiler_params=pltpu.CompilerParams(
+            collective_id=0, has_side_effects=True, vmem_limit_bytes=40 * 1024 * 1024
+        ),
+        cost_estimate=pl.CostEstimate(flops=2_000_000_000, bytes_accessed=3_000_000, transcendentals=600_000),
+    )(
+        patches,
+        norm_gain.reshape(1, chans),
+        w_first,
+        w_second,
+        depth_kernel.reshape(9, chans),
+        *[jnp.asarray(t) for t in tables],
+    )
+
+
+def fits(patches, w_first):
+    n_row, n_col = lax.axis_size("row"), lax.axis_size("col")
+    rows_dev, cols_dev, chans = patches.shape
+    blocks, width = w_first.shape[1:3]
+    half = cols_dev * n_col // 2
+    return (
+        blocks == n_col
+        and width == PAIR
+        and chans % LANES == 0
+        and rows_dev == 2 * TILE
+        and cols_dev % TILE == 0
+        and half == n_row * TILE
+    )
+
+
+def local(patches, norm_gain, w_first, w_second, depth_kernel):
+    plan = fused if fits(patches, w_first) else general
+    return plan(patches, norm_gain, w_first, w_second, depth_kernel)
+
+
 def solution(mesh):
     return jax.shard_map(
         local,

time: 186 us -> 90.7 us (0.49)
  waiting for transfers between devices: 98.1 us -> 0 us
  Pallas kernels: 0 us -> 81.9 us
  starting transfers between devices: 45.6 us -> 0 us
  other arithmetic: 18.8 us -> 0 us
  local copies, waits for them, and re-layouts: 15.5 us -> 8.4 us
  matrix products: 6.54 us -> 0 us
    all_to_all x10 -> x0, waiting for transfers between devices: 93.1 us -> none  [the longest x1 14.2 us: local(): lax.all_to_all(value_real, 'row', split_axis=0, concat_axis=1, tiled=True)]
    pallas_call x0 -> x1, Pallas kernels: none -> 81.9 us  [fused(): pl.pallas_call(functools.partial(mixing_kernel, n_row, n_col, 1.0 / math....]
    all_to_all x10 -> x0, starting transfers between devices: 39 us -> none  [the longest x1 5.16 us: local(): lax.all_to_all(normed, 'col', split_axis=0, concat_axis=1, tiled=True)]
    convert_element_type x5 -> x0, other arithmetic: 9.75 us -> none  [the longest x2 6.61 us: local(): return (xf + home.astype(jnp.float32) + conv).astype(jnp.bfloat16)]
    ppermute x4 -> x0, starting transfers between devices: 6.54 us -> none  [the longest x2 4.51 us: with_halo(): after = lax.ppermute(leading, axis, down)]
    dot_general x12 -> x0, matrix products: 6.54 us -> none  [the longest x8 4.15 us: block_product(): jnp.einsum('qmbc,bcd->qmbd', left, weight, preferred_element_type=jnp.flo...]
    unnamed x42 -> x17, local copies, waits for them, and re-layouts: 1.31 us -> 7.67 us
    slice x9 -> x0, local copies, waits for them, and re-layouts: 5.98 us -> none  [the longest x2 1.21 us: local(): wre = spectrum_values[:, :half]]
  transfers between devices with their start and end apart: 14 -> 0, of which waited for: 11 -> 0; matrix products, arithmetic and copies ran while one was open for 9% -> 0% of each run, Pallas kernels for 0% -> 0%
where the time goes in v1:
time: 90.7 us; the launch traced here: 90.3 us
  Pallas kernels  81.9 us (90%)
  local copies, waits for them, and re-layouts  8.4 us (9%)
    pallas_call x1, Pallas kernels, fused(): pl.pallas_call(functools.partial(mixing_kernel, n_row, n_col, 1.0 / math....  81.9 us
    unnamed x17, local copies, waits for them, and re-layouts  7.67 us

profile of v1, /device:TPU:0, one launch (start us, length us, event | category | flops | bytes accessed | tf_op | source)
XLA Modules:
  0.0 90.3 jit_solution(2862763036004887354)
XLA Ops:
  0.0 0.0 copy-start.3
  0.0 0.7 reshape.7.depth
  0.7 0.0 copy-done.3
  0.7 0.0 copy-start
  0.7 1.2 %copy-done = bf16[32,64,256]{2,1,0:T(8,128)(2,1)S(1)} copy-done((bf16[32,64,256]{2,1,0:T(8,128)(2,1)S(1)}, bf16[32,64,256]{2,1,0:T(8,128)(2,1)}, u32[]{:S(2)}) %copy-start) | copy-done | bytes 1048600
  2.0 0.0 copy-start.1
  2.0 0.9 copy-done.1
  2.9 0.0 copy-start.2
  2.9 0.9 copy-done.2
  3.8 0.0 copy-start.4
  3.8 0.9 %copy-done.4 = bf16[512,256]{1,0:T(8,128)(2,1)S(1)} copy-done((bf16[512,256]{1,0:T(8,128)(2,1)S(1)}, bf16[512,256]{1,0:T(8,128)(2,1)}, u32[]{:S(2)}) %copy-start.4) | copy-done | bytes 262168
  4.7 0.0 copy-start.5
  4.7 0.9 copy-done.5
  5.6 0.0 copy-start.6
  5.6 0.9 copy-done.6
  6.5 0.0 copy-start.7
  6.5 0.9 copy-done.7
  7.4 81.9 %shard_map.91 = bf16[32,64,256]{2,1,0:T(8,128)(2,1)S(1)} custom-call(bf16[32,64,256]{2,1,0:T(8,128)(2,1)S(1)} %copy-done, f32[1,256]{1,0:T(1,128)S(1)} %bitcast.1, bf16[2,4,64,64]{3,2,1,0:T(8,128)(2,1)S(1)} %copy-done.1, bf16[2,4,64,64]{3,2,1,0:T(8,128)(2,1)S(1)} %copy-done.2, f32[9,256]{1,0:T(8,128)S(1)} %reshape.7.depth, bf16[256,256]{1,0:T(8,128)(2,1)S(1)} %copy-done.7, ...), custom_call_target="tpu_custom_call" | custom-call | flops 2000000000 | bytes 3000000 | tf_op jit(solution)/shard_map/pallas_call | solution.py:550
  89.4 1.0 %copy.11 = bf16[32,64,256]{2,1,0:T(8,128)(2,1)} copy(bf16[32,64,256]{2,1,0:T(8,128)(2,1)S(1)} %shard_map.91) | data formatting | bytes 2097152
Async XLA Ops:
  0.0 0.7 copy-start.3
  0.7 1.2 %copy-start = (bf16[32,64,256]{2,1,0:T(8,128)(2,1)S(1)}, bf16[32,64,256]{2,1,0:T(8,128)(2,1)}, u32[]{:S(2)}) copy-start(bf16[32,64,256]{2,1,0:T(8,128)(2,1)} %patches.1) | copy-start | bytes 3145732
  2.0 0.9 %copy-start.1 = (bf16[2,4,64,64]{3,2,1,0:T(8,128)(2,1)S(1)}, bf16[2,4,64,64]{3,2,1,0:T(8,128)(2,1)}, u32[]{:S(2)}) copy-start(bf16[2,4,64,64]{3,2,1,0:T(8,128)(2,1)} %w_first.1) | copy-start | bytes 196612
  2.9 0.9 %copy-start.2 = (bf16[2,4,64,64]{3,2,1,0:T(8,128)(2,1)S(1)}, bf16[2,4,64,64]{3,2,1,0:T(8,128)(2,1)}, u32[]{:S(2)}) copy-start(bf16[2,4,64,64]{3,2,1,0:T(8,128)(2,1)} %w_second.1) | copy-start | bytes 196612
  3.8 0.9 %copy-start.4 = (bf16[512,256]{1,0:T(8,128)(2,1)S(1)}, bf16[512,256]{1,0:T(8,128)(2,1)}, u32[]{:S(2)}) copy-start(bf16[512,256]{1,0:T(8,128)(2,1)} %constant.10.clone.height_ref) | copy-start | bytes 786436
  4.7 0.9 %copy-start.5 = (bf16[256,256]{1,0:T(8,128)(2,1)S(1)}, bf16[256,256]{1,0:T(8,128)(2,1)}, u32[]{:S(2)}) copy-start(bf16[256,256]{1,0:T(8,128)(2,1)} %constant.11.clone.swap_ref) | copy-start | bytes 393220
  5.6 0.9 %copy-start.6 = (bf16[256,256]{1,0:T(8,128)(2,1)S(1)}, bf16[256,256]{1,0:T(8,128)(2,1)}, u32[]{:S(2)}) copy-start(bf16[256,256]{1,0:T(8,128)(2,1)} %constant.9.clone.inverse_ref) | copy-start | bytes 393220
  6.5 0.9 %copy-start.7 = (bf16[256,256]{1,0:T(8,128)(2,1)S(1)}, bf16[256,256]{1,0:T(8,128)(2,1)}, u32[]{:S(2)}) copy-start(bf16[256,256]{1,0:T(8,128)(2,1)} %constant.8.clone.forward_ref) | copy-start | bytes 393220

commit v2 on v1

--- a/solution.py
+++ b/solution.py
@@ -144,6 +144,7 @@
 TILE = 16
 COL_CHUNKS = 4
 KGROUPS = 2
+BATCH = 4
 
 
 def row_order(n_row, rows_dev):
@@ -156,6 +157,11 @@
             for slot in range(TILE):
                 order.append(s * rows_dev + (slot // per) * pairs + z * per + slot % per)
     return np.array(order)
+
+
+def exact_scale(length):
+    scale = 1.0 / math.sqrt(length)
+    return (scale, 1.0) if math.frexp(scale)[0] == 0.5 else (1.0, scale)
 
 
 def host_tables(grid_h, grid_w, n_row, rows_dev):
@@ -178,20 +184,30 @@
         for b in range(TILE):
             swap[a, b, b, a] = 1.0
     cast = lambda v: v.astype(ml_dtypes.bfloat16)
+    fold_w, fold_h = exact_scale(grid_w)[0], exact_scale(grid_h)[0]
     return (
-        cast(forward),
-        cast(inverse),
-        cast(np.concatenate([cos_h, sin_h], axis=0)),
+        cast(forward * fold_w),
+        cast(inverse * fold_w),
+        cast(np.concatenate([cos_h, sin_h], axis=0) * fold_h),
         cast(swap.reshape(TILE * TILE, TILE * TILE)),
     )
 
 
 def half_turn(x):
-    return pltpu.roll(x, PAIR, x.ndim - 1)
+    parts = [pltpu.roll(part, PAIR, 1) for part in lane_groups(x)]
+    return parts[0] if len(parts) == 1 else jnp.concatenate(parts, axis=1)
+
+
+def lane_groups(x):
+    return [x[:, i : i + LANES] for i in range(0, x.shape[1], LANES)]
 
 
 def low_lanes(shape):
-    return lax.broadcasted_iota(jnp.int32, shape, len(shape) - 1) < PAIR
+    return lax.broadcasted_iota(jnp.int32, shape, len(shape) - 1) % LANES < PAIR
+
+
+def scaled(x, factor):
+    return x if factor == 1.0 else x * factor
 
 
 def swap_halves(a, b):
@@ -204,6 +220,16 @@
     n_col,
     scale_w,
     scale_h,
+    patches_hbm,
+    gain_hbm,
+    w_first_hbm,
+    w_second_hbm,
+    depth_hbm,
+    forward_hbm,
+    inverse_hbm,
+    height_hbm,
+    swap_hbm,
+    out_hbm,
     patches,
     gain,
     w_first,
@@ -213,7 +239,6 @@
     inverse_ref,
     height_ref,
     swap_ref,
-    out,
     send1,
     recv1,
     turned,
@@ -237,6 +262,9 @@
     r4,
     sh,
     rh,
+    fetch_sem,
+    patch_sem,
+    out_sem,
 ):
     f32, bf16 = jnp.float32, jnp.bfloat16
     row, col = lax.axis_index("row"), lax.axis_index("col")
@@ -273,6 +301,40 @@
     for d in range(1, n_row):
         pl.semaphore_signal(barrier, inc=1, device_id=to_row(d), device_id_type=pl.DeviceIdType.MESH)
 
+    def chunk_rows(ch, side):
+        return pl.ds(side * pairs + ch * per_col, per_col)
+
+    def fetch_patches(ch, side):
+        rows = chunk_rows(ch, side)
+        return pltpu.make_async_copy(patches_hbm.at[rows], patches.at[rows], patch_sem.at[ch, side])
+
+    def leave(ch, side):
+        rows = chunk_rows(ch, side)
+        return pltpu.make_async_copy(patches.at[rows], out_hbm.at[rows], out_sem.at[ch, side])
+
+    operands = (
+        (gain_hbm, gain),
+        (forward_hbm, forward_ref),
+        (swap_hbm, swap_ref),
+        (w_first_hbm, w_first),
+        (w_second_hbm, w_second),
+        (depth_hbm, depth),
+        (height_hbm, height_ref),
+        (inverse_hbm, inverse_ref),
+    )
+    fetches = [
+        pltpu.make_async_copy(src, dst, fetch_sem.at[i]) for i, (src, dst) in enumerate(operands)
+    ]
+    for side in range(2):
+        fetch_patches(0, side).start()
+    fetches[0].start()
+    for ch in range(1, COL_CHUNKS):
+        for side in range(2):
+            fetch_patches(ch, side).start()
+    for fetch in fetches[1:]:
+        fetch.start()
+    fetches[0].wait()
+
     def copy1(ch, d):
         return pltpu.make_async_remote_copy(
             src_ref=send1.at[ch, col_peer(d)],
@@ -333,6 +395,8 @@
         return centred * lax.rsqrt(var + 1e-05) * gain[...]
 
     for ch in range(COL_CHUNKS):
+        for side in range(2):
+            fetch_patches(ch, side).wait()
 
         def norm_pair(i, carry, ch=ch):
             hp = ch * per_col + i
@@ -354,28 +418,33 @@
     def line(ch, i):
         return recv1[ch, :, i].reshape(grid_w, LANES)
 
+    for fetch in fetches[1:]:
+        fetch.wait()
     for z in range(zc):
         for ch in range(z * col_per_z, (z + 1) * col_per_z):
             for d in range(1, n_col):
                 copy1(ch, d).wait_recv()
 
-            def width_pair(i, carry, ch=ch, z=z):
-                y = dot(forward_ref[...], line(ch, i)) * scale_w
-                lower, upper = swap_halves(y[:half], y[half:])
+            x = jnp.concatenate([line(ch, i) for i in range(per_col)], axis=1)
+            y = scaled(dot(forward_ref[...], x), scale_w)
+            lower, upper = swap_halves(y[:half], y[half:])
+            for i in range(per_col):
                 slot = (ch - z * col_per_z) * per_col + i
-                turned[slot] = lower.astype(bf16)
-                turned[per_z + slot] = upper.astype(bf16)
-                return carry
-
-            lax.fori_loop(0, per_col, width_pair, 0)
-
-        def turn_out(r, carry, z=z):
-            ks = pl.ds(pl.multiple_of(r * kl, kl), kl)
-            tile = turned[:, ks, :].reshape(TILE * kl, LANES)
-            send2[z, r] = dot(swap_ref[...], tile).astype(bf16).reshape(kl, TILE, LANES)
+                turned[slot] = lane_groups(lower)[i].astype(bf16)
+                turned[per_z + slot] = lane_groups(upper)[i].astype(bf16)
+
+        def turn_out(step, carry, z=z):
+            rs = [step * BATCH + i for i in range(BATCH)]
+            tiles = [
+                turned[:, pl.ds(pl.multiple_of(r * kl, kl), kl), :].reshape(TILE * kl, LANES)
+                for r in rs
+            ]
+            swapped = dot(swap_ref[...], jnp.concatenate(tiles, axis=1)).astype(bf16)
+            for r, part in zip(rs, lane_groups(swapped)):
+                send2[z, r] = part.reshape(kl, TILE, LANES)
             return carry
 
-        lax.fori_loop(0, n_row, turn_out, 0)
+        lax.fori_loop(0, n_row // BATCH, turn_out, 0)
         for g in range(KGROUPS):
             for d in range(1, n_row):
                 copy2(z, g, d).start()
@@ -390,17 +459,25 @@
 
     def complex_weight(ref):
         re, im = ref[0, col].astype(f32), ref[1, col].astype(f32)
-        return jnp.concatenate(
+        one = jnp.concatenate(
             [jnp.concatenate([re, im], axis=1), jnp.concatenate([-im, re], axis=1)], axis=0
         ).astype(bf16)
+        none = jnp.zeros_like(one)
+        return jnp.concatenate(
+            [jnp.concatenate([one, none], axis=1), jnp.concatenate([none, one], axis=1)], axis=0
+        )
 
     weight_a, weight_b = complex_weight(w_first), complex_weight(w_second)
 
     lane_group = pl.multiple_of((col // 2) * LANES, LANES)
-    own = depth[:, pl.ds(lane_group, LANES)]
-    low = low_lanes(own.shape)
-    other = half_turn(own)
-    taps = jnp.where((col % 2) == 0, jnp.where(low, own, other), jnp.where(low, other, own))
+    taps = []
+    for i in range(3):
+        own = depth[i, :, pl.ds(lane_group, LANES)]
+        low = low_lanes(own.shape)
+        other = half_turn(own)
+        taps.append(
+            jnp.where((col % 2) == 0, jnp.where(low, own, other), jnp.where(low, other, own))
+        )
     for side in range(2):
         copy_rim(side).wait_recv()
     before = rim_recv[0].astype(f32)
@@ -416,7 +493,7 @@
         for j in range(3):
             part = None
             for i, rows in enumerate((above, here, below)):
-                term = rows * taps[3 * i + j : 3 * i + j + 1]
+                term = rows * taps[i][j : j + 1]
                 part = term if part is None else part + term
             if j == 0:
                 part = pltpu.roll(part, 1, 0)
@@ -437,31 +514,37 @@
     lax.fori_loop(1, pairs - 1, conv_inner, 0)
     conv_pair(pairs - 1, at(pairs - 2), at(pairs - 1), rim[1].astype(f32))
 
+    grid_h = rows_dev * n_row
+    sign = jnp.where(low_lanes((1, 2 * LANES)), 1.0, -1.0)
+
     def height(u):
         both = dot(height_ref[...], u)
-        n = both.shape[0] // 2
-        turned_part = half_turn(both[n:])
-        return both[:n], jnp.where(low_lanes(turned_part.shape), turned_part, -turned_part)
-
-    grid_h = rows_dev * n_row
-
-    def filter_mode(k, carry):
-        u = recv2[:, :, k].reshape(grid_h, LANES)
+        return both[:grid_h], half_turn(both[grid_h:]) * sign
+
+    def filter_pair(k):
+        u = jnp.concatenate(
+            [recv2[:, :, k + i].reshape(grid_h, LANES) for i in range(2)], axis=1
+        )
         a, b = height(u)
-        zed = ((a + b) * scale_h).astype(bf16)
+        zed = scaled(a + b, scale_h).astype(bf16)
         hidden = jnp.tanh(dot(zed, weight_a)).astype(bf16)
         s = dot(hidden, weight_b)
         s = (s - jnp.clip(s, -0.25, 0.25)).astype(bf16)
         a, b = height(s)
-        v = ((a - b) * scale_h).astype(bf16)
-        send3[:, :, k] = v.reshape(zc, n_row, TILE, LANES)
+        v = scaled(a - b, scale_h).astype(bf16)
+        for i, part in enumerate(lane_groups(v)):
+            send3[:, :, k + i] = part.reshape(zc, n_row, TILE, LANES)
+
+    def filter_modes(step, carry):
+        for i in range(0, BATCH, 2):
+            filter_pair(step * BATCH + i)
         return carry
 
     for g in range(KGROUPS):
         for z in range(zc):
             for d in range(1, n_row):
                 copy2(z, g, d).wait_recv()
-        lax.fori_loop(g * per_k, (g + 1) * per_k, filter_mode, 0)
+        lax.fori_loop(g * per_k // BATCH, (g + 1) * per_k // BATCH, filter_modes, 0)
         for d in range(1, n_row):
             copy3(0, g, d).start()
     for z in range(1, zc):
@@ -476,24 +559,26 @@
             for d in range(1, n_row):
                 copy3(z, g, d).wait_recv()
 
-        def turn_back(r, carry, z=z):
-            tile = recv3[z, r].reshape(kl * TILE, LANES)
-            ks = pl.ds(pl.multiple_of(r * kl, kl), kl)
-            turned[:, ks, :] = dot(swap_ref[...], tile).astype(bf16).reshape(TILE, kl, LANES)
+        def turn_back(step, carry, z=z):
+            rs = [step * BATCH + i for i in range(BATCH)]
+            tiles = [recv3[z, r].reshape(kl * TILE, LANES) for r in rs]
+            swapped = dot(swap_ref[...], jnp.concatenate(tiles, axis=1)).astype(bf16)
+            for r, part in zip(rs, lane_groups(swapped)):
+                ks = pl.ds(pl.multiple_of(r * kl, kl), kl)
+                turned[:, ks, :] = part.reshape(TILE, kl, LANES)
             return carry
 
-        lax.fori_loop(0, n_row, turn_back, 0)
+        lax.fori_loop(0, n_row // BATCH, turn_back, 0)
         for ch in range(z * col_per_z, (z + 1) * col_per_z):
-
-            def inverse_pair(i, carry, ch=ch, z=z):
+            columns = []
+            for i in range(per_col):
                 slot = (ch - z * col_per_z) * per_col + i
                 re, im = swap_halves(turned[slot].astype(f32), turned[per_z + slot].astype(f32))
-                x = jnp.concatenate([re.astype(bf16), im.astype(bf16)], axis=0)
-                cells = dot(inverse_ref[...], x) * scale_w + conv[ch * per_col + i]
-                send4[ch, :, i] = cells.astype(bf16).reshape(n_col, cols_dev, LANES)
-                return carry
-
-            lax.fori_loop(0, per_col, inverse_pair, 0)
+                columns.append(jnp.concatenate([re.astype(bf16), im.astype(bf16)], axis=0))
+            cells = scaled(dot(inverse_ref[...], jnp.concatenate(columns, axis=1)), scale_w)
+            for i, part in enumerate(lane_groups(cells)):
+                part = (part + conv[ch * per_col + i]).astype(bf16)
+                send4[ch, :, i] = part.reshape(n_col, cols_dev, LANES)
             for d in range(1, n_col):
                 copy4(ch, d).start()
             recv4[ch, col] = send4[ch, col]
@@ -509,13 +594,15 @@
                 lower, upper = swap_halves(
                     recv4[ch, 2 * j, i].astype(f32), recv4[ch, 2 * j + 1, i].astype(f32)
                 )
-                out[hp, :, lanes] = (patches[hp, :, lanes].astype(f32) + lower).astype(bf16)
-                out[hp + pairs, :, lanes] = (
+                patches[hp, :, lanes] = (patches[hp, :, lanes].astype(f32) + lower).astype(bf16)
+                patches[hp + pairs, :, lanes] = (
                     patches[hp + pairs, :, lanes].astype(f32) + upper
                 ).astype(bf16)
             return carry
 
         lax.fori_loop(0, per_col, finish_pair, 0)
+        for side in range(2):
+            leave(ch, side).start()
 
     for ch in range(COL_CHUNKS):
         for d in range(1, n_col):
@@ -528,6 +615,9 @@
                 copy3(z, g, d).wait_send()
     for side in range(2):
         copy_rim(side).wait_send()
+    for ch in range(COL_CHUNKS):
+        for side in range(2):
+            leave(ch, side).wait()
 
 
 def fused(patches, norm_gain, w_first, w_second, depth_kernel):
@@ -541,20 +631,29 @@
     kl = half // n_row
     tables = host_tables(grid_h, grid_w, n_row, rows_dev)
     bf16, f32 = jnp.bfloat16, jnp.float32
-    vmem = pl.BlockSpec(memory_space=pltpu.VMEM)
+    anywhere = pl.BlockSpec(memory_space=pl.ANY)
     col_buffer = pltpu.VMEM((COL_CHUNKS, n_col, per_col, cols_dev, LANES), bf16)
     row_buffer = pltpu.VMEM((zc, n_row, kl, TILE, LANES), bf16)
     col_sems = pltpu.SemaphoreType.DMA((COL_CHUNKS, n_col - 1))
     row_sems = pltpu.SemaphoreType.DMA((zc, KGROUPS, n_row - 1))
     rim_sems = pltpu.SemaphoreType.DMA((2,))
+    operands = (
+        patches,
+        norm_gain.reshape(1, chans),
+        w_first,
+        w_second,
+        depth_kernel,
+        *[jnp.asarray(t) for t in tables],
+    )
     return pl.pallas_call(
         functools.partial(
-            mixing_kernel, n_row, n_col, 1.0 / math.sqrt(grid_w), 1.0 / math.sqrt(grid_h)
+            mixing_kernel, n_row, n_col, exact_scale(grid_w)[1], exact_scale(grid_h)[1]
         ),
         out_shape=jax.ShapeDtypeStruct(patches.shape, bf16),
-        in_specs=[vmem] * 9,
-        out_specs=vmem,
+        in_specs=[anywhere] * 9,
+        out_specs=anywhere,
         scratch_shapes=[
+            *[pltpu.VMEM(v.shape, v.dtype) for v in operands],
             col_buffer,
             col_buffer,
             pltpu.VMEM((TILE, half, LANES), bf16),
@@ -578,19 +677,15 @@
             col_sems,
             rim_sems,
             rim_sems,
+            pltpu.SemaphoreType.DMA((8,)),
+            pltpu.SemaphoreType.DMA((COL_CHUNKS, 2)),
+            pltpu.SemaphoreType.DMA((COL_CHUNKS, 2)),
         ],
         compiler_params=pltpu.CompilerParams(
             collective_id=0, has_side_effects=True, vmem_limit_bytes=40 * 1024 * 1024
         ),
         cost_estimate=pl.CostEstimate(flops=2_000_000_000, bytes_accessed=3_000_000, transcendentals=600_000),
-    )(
-        patches,
-        norm_gain.reshape(1, chans),
-        w_first,
-        w_second,
-        depth_kernel.reshape(9, chans),
-        *[jnp.asarray(t) for t in tables],
-    )
+    )(*operands)
 
 
 def fits(patches, w_first):
@@ -605,6 +700,7 @@
         and rows_dev == 2 * TILE
         and cols_dev % TILE == 0
         and half == n_row * TILE
+        and n_row % BATCH == 0
     )
 
 

time: 90.7 us -> 83.6 us (0.922)
  Pallas kernels: 81.9 us -> 74.2 us
    pallas_call x1, Pallas kernels: 81.9 us -> 74.2 us  [fused(): pl.pallas_call(functools.partial(mixing_kernel, n_row, n_col, exact_scale...]
    unnamed x17 -> x19, local copies, waits for them, and re-layouts: 7.67 us -> 9.05 us
where the time goes in v2:
time: 83.6 us; the launch traced here: 83.2 us
  Pallas kernels  74.2 us (89%)
  local copies, waits for them, and re-layouts  9.05 us (11%)
    pallas_call x1, Pallas kernels, fused(): pl.pallas_call(functools.partial(mixing_kernel, n_row, n_col, exact_scale...  74.2 us
    unnamed x19, local copies, waits for them, and re-layouts  9.05 us

profile of v2, /device:TPU:0, one launch (start us, length us, event | category | flops | bytes accessed | tf_op | source)
XLA Modules:
  0.0 83.2 jit_solution(13450624315802567859)
XLA Ops:
  0.0 0.0 copy-start.4
  0.0 0.7 copy-done.4
  0.7 0.0 copy-start
  0.7 1.2 %copy-done = bf16[32,64,256]{2,1,0:T(8,128)(2,1)S(1)} copy-done((bf16[32,64,256]{2,1,0:T(8,128)(2,1)S(1)}, bf16[32,64,256]{2,1,0:T(8,128)(2,1)}, u32[]{:S(2)}) %copy-start) | copy-done | bytes 1048600
  1.9 0.0 copy-start.1
  1.9 0.9 %copy-done.1 = bf16[2,4,64,64]{3,2,1,0:T(8,128)(2,1)S(1)} copy-done((bf16[2,4,64,64]{3,2,1,0:T(8,128)(2,1)S(1)}, bf16[2,4,64,64]{3,2,1,0:T(8,128)(2,1)}, u32[]{:S(2)}) %copy-start.1) | copy-done | bytes 65560
  2.8 0.0 copy-start.2
  2.8 0.9 %copy-done.2 = bf16[2,4,64,64]{3,2,1,0:T(8,128)(2,1)S(1)} copy-done((bf16[2,4,64,64]{3,2,1,0:T(8,128)(2,1)S(1)}, bf16[2,4,64,64]{3,2,1,0:T(8,128)(2,1)}, u32[]{:S(2)}) %copy-start.2) | copy-done | bytes 65560
  3.7 0.0 copy-start.3
  3.7 0.7 copy-done.3
  4.4 0.0 copy-start.5
  4.4 0.9 %copy-done.5 = bf16[512,256]{1,0:T(8,128)(2,1)S(1)} copy-done((bf16[512,256]{1,0:T(8,128)(2,1)S(1)}, bf16[512,256]{1,0:T(8,128)(2,1)}, u32[]{:S(2)}) %copy-start.5) | copy-done | bytes 262168
  5.4 0.0 copy-start.6
  5.4 0.9 %copy-done.6 = bf16[256,256]{1,0:T(8,128)(2,1)S(1)} copy-done((bf16[256,256]{1,0:T(8,128)(2,1)S(1)}, bf16[256,256]{1,0:T(8,128)(2,1)}, u32[]{:S(2)}) %copy-start.6) | copy-done | bytes 131096
  6.3 0.0 copy-start.7
  6.3 0.9 %copy-done.7 = bf16[256,256]{1,0:T(8,128)(2,1)S(1)} copy-done((bf16[256,256]{1,0:T(8,128)(2,1)S(1)}, bf16[256,256]{1,0:T(8,128)(2,1)}, u32[]{:S(2)}) %copy-start.7) | copy-done | bytes 131096
  7.2 0.0 copy-start.8
  7.2 0.9 %copy-done.8 = bf16[256,256]{1,0:T(8,128)(2,1)S(1)} copy-done((bf16[256,256]{1,0:T(8,128)(2,1)S(1)}, bf16[256,256]{1,0:T(8,128)(2,1)}, u32[]{:S(2)}) %copy-start.8) | copy-done | bytes 131096
  8.1 74.2 %shard_map.91 = bf16[32,64,256]{2,1,0:T(8,128)(2,1)S(1)} custom-call(bf16[32,64,256]{2,1,0:T(8,128)(2,1)S(1)} %copy-done, f32[1,256]{1,0:T(1,128)S(1)} %bitcast.1, bf16[2,4,64,64]{3,2,1,0:T(8,128)(2,1)S(1)} %copy-done.1, bf16[2,4,64,64]{3,2,1,0:T(8,128)(2,1)S(1)} %copy-done.2, f32[3,3,256]{2,1,0:T(4,128)S(1)} %copy-done.3, bf16[256,256]{1,0:T(8,128)(2,1)S(1)} %copy-done.8, ...), custom_call_target="tpu_custom_call" | custom-call | flops 2000000000 | bytes 3000000 | tf_op jit(solution)/shard_map/pallas_call | solution.py:648
  82.3 1.0 %copy.11 = bf16[32,64,256]{2,1,0:T(8,128)(2,1)} copy(bf16[32,64,256]{2,1,0:T(8,128)(2,1)S(1)} %shard_map.91) | data formatting | bytes 2097152
Async XLA Ops:
  0.0 0.7 copy-start.4
  0.7 1.2 %copy-start = (bf16[32,64,256]{2,1,0:T(8,128)(2,1)S(1)}, bf16[32,64,256]{2,1,0:T(8,128)(2,1)}, u32[]{:S(2)}) copy-start(bf16[32,64,256]{2,1,0:T(8,128)(2,1)} %patches_hbm.1) | copy-start | bytes 3145732
  1.9 0.9 %copy-start.1 = (bf16[2,4,64,64]{3,2,1,0:T(8,128)(2,1)S(1)}, bf16[2,4,64,64]{3,2,1,0:T(8,128)(2,1)}, u32[]{:S(2)}) copy-start(bf16[2,4,64,64]{3,2,1,0:T(8,128)(2,1)} %w_first_hbm.1) | copy-start | bytes 196612
  2.8 0.9 %copy-start.2 = (bf16[2,4,64,64]{3,2,1,0:T(8,128)(2,1)S(1)}, bf16[2,4,64,64]{3,2,1,0:T(8,128)(2,1)}, u32[]{:S(2)}) copy-start(bf16[2,4,64,64]{3,2,1,0:T(8,128)(2,1)} %w_second_hbm.1) | copy-start | bytes 196612
  3.7 0.7 copy-start.3
  4.4 0.9 %copy-start.5 = (bf16[512,256]{1,0:T(8,128)(2,1)S(1)}, bf16[512,256]{1,0:T(8,128)(2,1)}, u32[]{:S(2)}) copy-start(bf16[512,256]{1,0:T(8,128)(2,1)} %constant.10.clone.height_hbm) | copy-start | bytes 786436
  5.4 0.9 %copy-start.6 = (bf16[256,256]{1,0:T(8,128)(2,1)S(1)}, bf16[256,256]{1,0:T(8,128)(2,1)}, u32[]{:S(2)}) copy-start(bf16[256,256]{1,0:T(8,128)(2,1)} %constant.11.clone.swap_hbm) | copy-start | bytes 393220
  6.3 0.9 %copy-start.7 = (bf16[256,256]{1,0:T(8,128)(2,1)S(1)}, bf16[256,256]{1,0:T(8,128)(2,1)}, u32[]{:S(2)}) copy-start(bf16[256,256]{1,0:T(8,128)(2,1)} %constant.9.clone.inverse_hbm) | copy-start | bytes 393220
  7.2 0.9 %copy-start.8 = (bf16[256,256]{1,0:T(8,128)(2,1)S(1)}, bf16[256,256]{1,0:T(8,128)(2,1)}, u32[]{:S(2)}) copy-start(bf16[256,256]{1,0:T(8,128)(2,1)} %constant.8.clone.forward_hbm) | copy-start | bytes 393220

commit v3 on v2

--- a/solution.py
+++ b/solution.py
@@ -142,19 +142,21 @@
 LANES = 128
 PAIR = 64
 TILE = 16
+SLOTS = 8
+TURN = 32
 COL_CHUNKS = 4
 KGROUPS = 2
-BATCH = 4
+BATCH = 2
 
 
 def row_order(n_row, rows_dev):
     pairs = rows_dev // 2
-    zc = rows_dev // TILE
+    zc = rows_dev // SLOTS
     per = pairs // zc
     order = []
     for z in range(zc):
         for s in range(n_row):
-            for slot in range(TILE):
+            for slot in range(SLOTS):
                 order.append(s * rows_dev + (slot // per) * pairs + z * per + slot % per)
     return np.array(order)
 
@@ -179,17 +181,18 @@
     inverse = np.concatenate([cos_w * weight, -sin_w * weight], axis=0).T
     order = row_order(n_row, rows_dev)
     cos_h, sin_h = table(order, order, grid_h)
-    swap = np.zeros((TILE, TILE, TILE, TILE), np.float32)
-    for a in range(TILE):
-        for b in range(TILE):
+    swap = np.zeros((TURN, SLOTS, SLOTS, TURN), np.float32)
+    for a in range(TURN):
+        for b in range(SLOTS):
             swap[a, b, b, a] = 1.0
+    swap = swap.reshape(TURN * SLOTS, TURN * SLOTS)
     cast = lambda v: v.astype(ml_dtypes.bfloat16)
     fold_w, fold_h = exact_scale(grid_w)[0], exact_scale(grid_h)[0]
     return (
         cast(forward * fold_w),
         cast(inverse * fold_w),
         cast(np.concatenate([cos_h, sin_h], axis=0) * fold_h),
-        cast(swap.reshape(TILE * TILE, TILE * TILE)),
+        cast(np.stack([swap, swap.T])),
     )
 
 
@@ -271,13 +274,13 @@
     rows_dev, cols_dev, chans = patches.shape
     pairs = rows_dev // 2
     per_col = pairs // COL_CHUNKS
-    zc = rows_dev // TILE
-    per_z = pairs // zc
-    col_per_z = COL_CHUNKS // zc
+    zc = COL_CHUNKS
     grid_w = cols_dev * n_col
     half = grid_w // 2
     kl = half // n_row
-    per_k = kl // KGROUPS
+    per_k = kl // 2 // KGROUPS
+    turns = [pl.ds(q * TURN, TURN) for q in range(half // TURN)]
+    owners = [pl.ds(q * TURN // kl, TURN // kl) for q in range(half // TURN)]
     groups = chans // LANES
 
     def col_peer(d):
@@ -421,30 +424,18 @@
     for fetch in fetches[1:]:
         fetch.wait()
     for z in range(zc):
-        for ch in range(z * col_per_z, (z + 1) * col_per_z):
-            for d in range(1, n_col):
-                copy1(ch, d).wait_recv()
-
-            x = jnp.concatenate([line(ch, i) for i in range(per_col)], axis=1)
-            y = scaled(dot(forward_ref[...], x), scale_w)
-            lower, upper = swap_halves(y[:half], y[half:])
-            for i in range(per_col):
-                slot = (ch - z * col_per_z) * per_col + i
-                turned[slot] = lane_groups(lower)[i].astype(bf16)
-                turned[per_z + slot] = lane_groups(upper)[i].astype(bf16)
-
-        def turn_out(step, carry, z=z):
-            rs = [step * BATCH + i for i in range(BATCH)]
-            tiles = [
-                turned[:, pl.ds(pl.multiple_of(r * kl, kl), kl), :].reshape(TILE * kl, LANES)
-                for r in rs
-            ]
-            swapped = dot(swap_ref[...], jnp.concatenate(tiles, axis=1)).astype(bf16)
-            for r, part in zip(rs, lane_groups(swapped)):
-                send2[z, r] = part.reshape(kl, TILE, LANES)
-            return carry
-
-        lax.fori_loop(0, n_row // BATCH, turn_out, 0)
+        for d in range(1, n_col):
+            copy1(z, d).wait_recv()
+        x = jnp.concatenate([line(z, i) for i in range(per_col)], axis=1)
+        y = scaled(dot(forward_ref[...], x), scale_w)
+        lower, upper = swap_halves(y[:half], y[half:])
+        for i in range(per_col):
+            turned[i] = lane_groups(lower)[i].astype(bf16)
+            turned[per_col + i] = lane_groups(upper)[i].astype(bf16)
+        tiles = [turned[:, ks, :].reshape(TURN * SLOTS, LANES) for ks in turns]
+        swapped = dot(swap_ref[0], jnp.concatenate(tiles, axis=1)).astype(bf16)
+        for own, part in zip(owners, lane_groups(swapped)):
+            send2[z, own] = part.reshape(TURN // kl, kl // 2, TILE, LANES)
         for g in range(KGROUPS):
             for d in range(1, n_row):
                 copy2(z, g, d).start()
@@ -522,8 +513,13 @@
         return both[:grid_h], half_turn(both[grid_h:]) * sign
 
     def filter_pair(k):
+        tile = recv2[:, :, k].astype(f32).reshape(zc * n_row, TILE, LANES)
         u = jnp.concatenate(
-            [recv2[:, :, k + i].reshape(grid_h, LANES) for i in range(2)], axis=1
+            [
+                tile[:, i : i + SLOTS].reshape(grid_h, LANES).astype(bf16)
+                for i in range(0, TILE, SLOTS)
+            ],
+            axis=1,
         )
         a, b = height(u)
         zed = scaled(a + b, scale_h).astype(bf16)
@@ -531,12 +527,12 @@
         s = dot(hidden, weight_b)
         s = (s - jnp.clip(s, -0.25, 0.25)).astype(bf16)
         a, b = height(s)
-        v = scaled(a - b, scale_h).astype(bf16)
-        for i, part in enumerate(lane_groups(v)):
-            send3[:, :, k + i] = part.reshape(zc, n_row, TILE, LANES)
+        v = lane_groups(scaled(a - b, scale_h))
+        v = jnp.concatenate([part.reshape(zc * n_row, SLOTS, LANES) for part in v], axis=1)
+        send3[:, :, k] = v.astype(bf16).reshape(zc, n_row, TILE, LANES)
 
     def filter_modes(step, carry):
-        for i in range(0, BATCH, 2):
+        for i in range(BATCH):
             filter_pair(step * BATCH + i)
         return carry
 
@@ -559,29 +555,21 @@
             for d in range(1, n_row):
                 copy3(z, g, d).wait_recv()
 
-        def turn_back(step, carry, z=z):
-            rs = [step * BATCH + i for i in range(BATCH)]
-            tiles = [recv3[z, r].reshape(kl * TILE, LANES) for r in rs]
-            swapped = dot(swap_ref[...], jnp.concatenate(tiles, axis=1)).astype(bf16)
-            for r, part in zip(rs, lane_groups(swapped)):
-                ks = pl.ds(pl.multiple_of(r * kl, kl), kl)
-                turned[:, ks, :] = part.reshape(TILE, kl, LANES)
-            return carry
-
-        lax.fori_loop(0, n_row // BATCH, turn_back, 0)
-        for ch in range(z * col_per_z, (z + 1) * col_per_z):
-            columns = []
-            for i in range(per_col):
-                slot = (ch - z * col_per_z) * per_col + i
-                re, im = swap_halves(turned[slot].astype(f32), turned[per_z + slot].astype(f32))
-                columns.append(jnp.concatenate([re.astype(bf16), im.astype(bf16)], axis=0))
-            cells = scaled(dot(inverse_ref[...], jnp.concatenate(columns, axis=1)), scale_w)
-            for i, part in enumerate(lane_groups(cells)):
-                part = (part + conv[ch * per_col + i]).astype(bf16)
-                send4[ch, :, i] = part.reshape(n_col, cols_dev, LANES)
-            for d in range(1, n_col):
-                copy4(ch, d).start()
-            recv4[ch, col] = send4[ch, col]
+        tiles = [recv3[z, own].reshape(TURN * SLOTS, LANES) for own in owners]
+        swapped = dot(swap_ref[1], jnp.concatenate(tiles, axis=1)).astype(bf16)
+        for ks, part in zip(turns, lane_groups(swapped)):
+            turned[:, ks, :] = part.reshape(SLOTS, TURN, LANES)
+        columns = []
+        for i in range(per_col):
+            re, im = swap_halves(turned[i].astype(f32), turned[per_col + i].astype(f32))
+            columns.append(jnp.concatenate([re.astype(bf16), im.astype(bf16)], axis=0))
+        cells = scaled(dot(inverse_ref[...], jnp.concatenate(columns, axis=1)), scale_w)
+        for i, part in enumerate(lane_groups(cells)):
+            part = (part + conv[z * per_col + i]).astype(bf16)
+            send4[z, :, i] = part.reshape(n_col, cols_dev, LANES)
+        for d in range(1, n_col):
+            copy4(z, d).start()
+        recv4[z, col] = send4[z, col]
 
     for ch in range(COL_CHUNKS):
         for d in range(1, n_col):
@@ -625,15 +613,15 @@
     n_col = lax.axis_size("col")
     rows_dev, cols_dev, chans = patches.shape
     grid_h, grid_w = rows_dev * n_row, cols_dev * n_col
-    pairs, zc = rows_dev // 2, rows_dev // TILE
+    pairs, zc = rows_dev // 2, COL_CHUNKS
     per_col = pairs // COL_CHUNKS
     half = grid_w // 2
     kl = half // n_row
     tables = host_tables(grid_h, grid_w, n_row, rows_dev)
     bf16, f32 = jnp.bfloat16, jnp.float32
-    anywhere = pl.BlockSpec(memory_space=pl.ANY)
+    anywhere = pl.BlockSpec(memory_space=pltpu.HBM)
     col_buffer = pltpu.VMEM((COL_CHUNKS, n_col, per_col, cols_dev, LANES), bf16)
-    row_buffer = pltpu.VMEM((zc, n_row, kl, TILE, LANES), bf16)
+    row_buffer = pltpu.VMEM((zc, n_row, kl // 2, TILE, LANES), bf16)
     col_sems = pltpu.SemaphoreType.DMA((COL_CHUNKS, n_col - 1))
     row_sems = pltpu.SemaphoreType.DMA((zc, KGROUPS, n_row - 1))
     rim_sems = pltpu.SemaphoreType.DMA((2,))
@@ -656,7 +644,7 @@
             *[pltpu.VMEM(v.shape, v.dtype) for v in operands],
             col_buffer,
             col_buffer,
-            pltpu.VMEM((TILE, half, LANES), bf16),
+            pltpu.VMEM((SLOTS, half, LANES), bf16),
             row_buffer,
             row_buffer,
             row_buffer,
@@ -682,7 +670,7 @@
             pltpu.SemaphoreType.DMA((COL_CHUNKS, 2)),
         ],
         compiler_params=pltpu.CompilerParams(
-            collective_id=0, has_side_effects=True, vmem_limit_bytes=40 * 1024 * 1024
+            collective_id=0, has_side_effects=True, vmem_limit_bytes=62 * 1024 * 1024
         ),
         cost_estimate=pl.CostEstimate(flops=2_000_000_000, bytes_accessed=3_000_000, transcendentals=600_000),
     )(*operands)
@@ -697,10 +685,10 @@
         blocks == n_col
         and width == PAIR
         and chans % LANES == 0
-        and rows_dev == 2 * TILE
+        and rows_dev == COL_CHUNKS * SLOTS
         and cols_dev % TILE == 0
         and half == n_row * TILE
-        and n_row % BATCH == 0
+        and half % TURN == 0
     )
 
 

time: 83.6 us -> 74.5 us (0.89)
  local copies, waits for them, and re-layouts: 9.05 us -> 2.3 us
  Pallas kernels: 74.2 us -> 72.1 us
    unnamed x19 -> x1, local copies, waits for them, and re-layouts: 9.05 us -> 2.3 us
    pallas_call x1, Pallas kernels: 74.2 us -> 72.1 us  [fused(): pl.pallas_call(functools.partial(mixing_kernel, n_row, n_col, exact_scale...]
where the time goes in v3:
time: 74.5 us; the launch traced here: 74.4 us
  Pallas kernels  72.1 us (97%)
  local copies, waits for them, and re-layouts  2.3 us (3%)
    pallas_call x1, Pallas kernels, fused(): pl.pallas_call(functools.partial(mixing_kernel, n_row, n_col, exact_scale...  72.1 us
    unnamed x1, local copies, waits for them, and re-layouts  2.3 us

profile of v3, /device:TPU:0, one launch (start us, length us, event | category | flops | bytes accessed | tf_op | source)
XLA Modules:
  0.0 74.4 jit_solution(10608187722915398697)
XLA Ops:
  0.0 72.1 %shard_map.91 = bf16[32,64,256]{2,1,0:T(8,128)(2,1)} custom-call(bf16[32,64,256]{2,1,0:T(8,128)(2,1)} %patches_hbm.1, f32[1,256]{1,0:T(1,128)} %bitcast.1, bf16[2,4,64,64]{3,2,1,0:T(8,128)(2,1)} %w_first_hbm.1, bf16[2,4,64,64]{3,2,1,0:T(8,128)(2,1)} %w_second_hbm.1, f32[3,3,256]{2,1,0:T(4,128)} %depth_hbm.1, bf16[256,256]{1,0:T(8,128)(2,1)} %constant.8.clone.forward_hbm, ...), custom_call_target="tpu_custom_call" | custom-call | flops 2000000000 | bytes 3000000 | tf_op jit(solution)/shard_map/pallas_call | solution.py:636
  72.1 2.3 %copy.11 = bf16[32,64,256]{2,1,0:T(8,128)(2,1)} copy(bf16[32,64,256]{2,1,0:T(8,128)(2,1)} %shard_map.91) | data formatting | bytes 2097152

commit v4 on v3

--- a/solution.py
+++ b/solution.py
@@ -287,7 +287,19 @@
         return lax.rem(col + d, n_col)
 
     def row_peer(d):
-        return lax.rem(row + d, n_row)
+        bits, peer, weight = d, 0, 1
+        while weight < n_row:
+            own = lax.rem(row // weight, 2)
+            peer = peer + weight * (1 - own if bits % 2 else own)
+            bits, weight = bits // 2, 2 * weight
+        return peer
+
+    near = list(range(1, n_row // 2))
+    row_order_of = []
+    for d in range(n_row // 2, n_row):
+        row_order_of.append(d)
+        if near:
+            row_order_of.append(near.pop(0))
 
     def to_col(d):
         return {"col": col_peer(d)}
@@ -386,7 +398,7 @@
             dst_ref=rim_recv.at[side],
             send_sem=sh.at[side],
             recv_sem=rh.at[side],
-            device_id=to_row(1 if side == 0 else n_row - 1),
+            device_id={"row": lax.rem(row + (1 if side == 0 else n_row - 1), n_row)},
             device_id_type=pl.DeviceIdType.MESH,
         )
 
@@ -437,7 +449,7 @@
         for own, part in zip(owners, lane_groups(swapped)):
             send2[z, own] = part.reshape(TURN // kl, kl // 2, TILE, LANES)
         for g in range(KGROUPS):
-            for d in range(1, n_row):
+            for d in row_order_of:
                 copy2(z, g, d).start()
         recv2[z, row] = send2[z, row]
 
@@ -469,16 +481,6 @@
         taps.append(
             jnp.where((col % 2) == 0, jnp.where(low, own, other), jnp.where(low, other, own))
         )
-    for side in range(2):
-        copy_rim(side).wait_recv()
-    before = rim_recv[0].astype(f32)
-    after = rim_recv[1].astype(f32)
-    before = jnp.concatenate([before, half_turn(before)], axis=0)
-    after = jnp.concatenate([half_turn(after), after], axis=0)
-    low = low_lanes(before.shape)
-    rim[0] = jnp.where(low, before, half_turn(final)).astype(bf16)
-    rim[1] = jnp.where(low, half_turn(first), after).astype(bf16)
-
     def conv_pair(hp, above, here, below):
         total = None
         for j in range(3):
@@ -496,14 +498,11 @@
     def at(hp):
         return line(hp // per_col, hp % per_col).astype(f32)
 
-    conv_pair(0, rim[0].astype(f32), at(0), at(1))
-
     def conv_inner(hp, carry):
         conv_pair(hp, at(hp - 1), at(hp), at(hp + 1))
         return carry
 
     lax.fori_loop(1, pairs - 1, conv_inner, 0)
-    conv_pair(pairs - 1, at(pairs - 2), at(pairs - 1), rim[1].astype(f32))
 
     grid_h = rows_dev * n_row
     sign = jnp.where(low_lanes((1, 2 * LANES)), 1.0, -1.0)
@@ -541,14 +540,27 @@
             for d in range(1, n_row):
                 copy2(z, g, d).wait_recv()
         lax.fori_loop(g * per_k // BATCH, (g + 1) * per_k // BATCH, filter_modes, 0)
-        for d in range(1, n_row):
+        for d in row_order_of:
             copy3(0, g, d).start()
     for z in range(1, zc):
         for g in range(KGROUPS):
-            for d in range(1, n_row):
+            for d in row_order_of:
                 copy3(z, g, d).start()
     for z in range(zc):
         recv3[z, row] = send3[z, row]
+
+    for side in range(2):
+        copy_rim(side).wait_recv()
+    before = rim_recv[0].astype(f32)
+    after = rim_recv[1].astype(f32)
+    before = jnp.concatenate([before, half_turn(before)], axis=0)
+    after = jnp.concatenate([half_turn(after), after], axis=0)
+    low = low_lanes(before.shape)
+    rim[0] = jnp.where(low, before, half_turn(at(pairs - 1))).astype(bf16)
+    rim[1] = jnp.where(low, half_turn(at(0)), after).astype(bf16)
+
+    conv_pair(0, rim[0].astype(f32), at(0), at(1))
+    conv_pair(pairs - 1, at(pairs - 2), at(pairs - 1), rim[1].astype(f32))
 
     for z in range(zc):
         for g in range(KGROUPS):
@@ -582,10 +594,8 @@
                 lower, upper = swap_halves(
                     recv4[ch, 2 * j, i].astype(f32), recv4[ch, 2 * j + 1, i].astype(f32)
                 )
-                patches[hp, :, lanes] = (patches[hp, :, lanes].astype(f32) + lower).astype(bf16)
-                patches[hp + pairs, :, lanes] = (
-                    patches[hp + pairs, :, lanes].astype(f32) + upper
-                ).astype(bf16)
+                patches[hp, :, lanes] = lower.astype(bf16)
+                patches[hp + pairs, :, lanes] = upper.astype(bf16)
             return carry
 
         lax.fori_loop(0, per_col, finish_pair, 0)
@@ -633,7 +643,7 @@
         depth_kernel,
         *[jnp.asarray(t) for t in tables],
     )
-    return pl.pallas_call(
+    branches = pl.pallas_call(
         functools.partial(
             mixing_kernel, n_row, n_col, exact_scale(grid_w)[1], exact_scale(grid_h)[1]
         ),
@@ -674,6 +684,7 @@
         ),
         cost_estimate=pl.CostEstimate(flops=2_000_000_000, bytes_accessed=3_000_000, transcendentals=600_000),
     )(*operands)
+    return (patches.astype(f32) + branches.astype(f32)).astype(bf16)
 
 
 def fits(patches, w_first):
@@ -689,6 +700,7 @@
         and cols_dev % TILE == 0
         and half == n_row * TILE
         and half % TURN == 0
+        and n_row & (n_row - 1) == 0
     )
 
 

time: 74.5 us -> 73.5 us (0.987)
  other arithmetic: 0 us -> 2.61 us
  local copies, waits for them, and re-layouts: 2.3 us -> 0.01 us
  Pallas kernels: 72.1 us -> 70.7 us
    convert_element_type x0 -> x1, other arithmetic: none -> 2.61 us  [fused(): return (patches.astype(f32) + branches.astype(f32)).astype(bf16)]
    unnamed x1 -> x2, local copies, waits for them, and re-layouts: 2.3 us -> 0.01 us
    pallas_call x1, Pallas kernels: 72.1 us -> 70.7 us  [fused(): pl.pallas_call(functools.partial(mixing_kernel, n_row, n_col, exact_scale...]
where the time goes in v4:
time: 73.5 us; the launch traced here: 73.4 us
  Pallas kernels  70.7 us (96%)
  other arithmetic  2.61 us (4%)
    pallas_call x1, Pallas kernels, fused(): pl.pallas_call(functools.partial(mixing_kernel, n_row, n_col, exact_scale...  70.7 us
    convert_element_type x1, other arithmetic, fused(): return (patches.astype(f32) + branches.astype(f32)).astype(bf16)  2.61 us

profile of v4, /device:TPU:0, one launch (start us, length us, event | category | flops | bytes accessed | tf_op | source)
XLA Modules:
  0.0 73.4 jit_solution(4032529164419292926)
XLA Ops:
  0.0 0.0 copy-start
  0.0 70.7 %shard_map.91 = bf16[32,64,256]{2,1,0:T(8,128)(2,1)} custom-call(bf16[32,64,256]{2,1,0:T(8,128)(2,1)} %patches_hbm.1, f32[1,256]{1,0:T(1,128)} %bitcast.1, bf16[2,4,64,64]{3,2,1,0:T(8,128)(2,1)} %w_first_hbm.1, bf16[2,4,64,64]{3,2,1,0:T(8,128)(2,1)} %w_second_hbm.1, f32[3,3,256]{2,1,0:T(4,128)} %depth_hbm.1, bf16[256,256]{1,0:T(8,128)(2,1)} %constant.8.clone.forward_hbm, ...), custom_call_target="tpu_custom_call" | custom-call | flops 2000000000 | bytes 3000000 | tf_op jit(solution)/shard_map/pallas_call | solution.py:646
  70.7 0.0 copy-done
  70.8 2.6 %add_convert_fusion = bf16[32,64,256]{2,1,0:T(8,128)(2,1)} fusion(bf16[32,64,256]{2,1,0:T(8,128)(2,1)} %shard_map.91, bf16[32,64,256]{2,1,0:T(8,128)(2,1)S(1)} %copy-done), kind=kLoop, calls=%fused_computation | loop fusion | flops 2097152 | bytes 3145728 | tf_op jit(solution)/shard_map/convert_element_type | solution.py:687
Async XLA Ops:
  0.0 70.8 %copy-start = (bf16[32,64,256]{2,1,0:T(8,128)(2,1)S(1)}, bf16[32,64,256]{2,1,0:T(8,128)(2,1)}, u32[]{:S(2)}) copy-start(bf16[32,64,256]{2,1,0:T(8,128)(2,1)} %patches_hbm.1) | copy-start | bytes 3145732

commit v5 on v4

--- a/solution.py
+++ b/solution.py
@@ -409,11 +409,11 @@
         var = jnp.mean(centred * centred, axis=-1, keepdims=True)
         return centred * lax.rsqrt(var + 1e-05) * gain[...]
 
-    for ch in range(COL_CHUNKS):
+    def norm_chunk(ch):
         for side in range(2):
             fetch_patches(ch, side).wait()
 
-        def norm_pair(i, carry, ch=ch):
+        def norm_pair(i, carry):
             hp = ch * per_col + i
             lower, upper = normed_row(hp), normed_row(hp + pairs)
             for j in range(groups):
@@ -423,12 +423,15 @@
                 send1[ch, 2 * j + 1, i] = odd.astype(bf16)
             return carry
 
-        lax.fori_loop(0, per_col, norm_pair, 0)
+        lax.fori_loop(0, per_col, norm_pair, 0, unroll=2)
         if ch == 0:
             pl.semaphore_wait(barrier, n_col + n_row - 2)
         for d in range(1, n_col):
             copy1(ch, d).start()
         recv1[ch, col] = send1[ch, col]
+
+    norm_chunk(0)
+    norm_chunk(1)
 
     def line(ch, i):
         return recv1[ch, :, i].reshape(grid_w, LANES)
@@ -452,6 +455,8 @@
             for d in row_order_of:
                 copy2(z, g, d).start()
         recv2[z, row] = send2[z, row]
+        if z + 2 < COL_CHUNKS:
+            norm_chunk(z + 2)
 
     first = line(0, 0).astype(f32)
     final = line(COL_CHUNKS - 1, per_col - 1).astype(f32)
@@ -562,6 +567,27 @@
     conv_pair(0, rim[0].astype(f32), at(0), at(1))
     conv_pair(pairs - 1, at(pairs - 2), at(pairs - 1), rim[1].astype(f32))
 
+    def finish(ch):
+        for d in range(1, n_col):
+            copy4(ch, d).wait_recv()
+
+        def finish_pair(i, carry):
+            hp = ch * per_col + i
+            for j in range(groups):
+                lanes = slice(j * LANES, (j + 1) * LANES)
+                lower, upper = swap_halves(
+                    recv4[ch, 2 * j, i].astype(f32), recv4[ch, 2 * j + 1, i].astype(f32)
+                )
+                patches[hp, :, lanes] = (patches[hp, :, lanes].astype(f32) + lower).astype(bf16)
+                patches[hp + pairs, :, lanes] = (
+                    patches[hp + pairs, :, lanes].astype(f32) + upper
+                ).astype(bf16)
+            return carry
+
+        lax.fori_loop(0, per_col, finish_pair, 0, unroll=2)
+        for side in range(2):
+            leave(ch, side).start()
+
     for z in range(zc):
         for g in range(KGROUPS):
             for d in range(1, n_row):
@@ -582,25 +608,10 @@
         for d in range(1, n_col):
             copy4(z, d).start()
         recv4[z, col] = send4[z, col]
-
-    for ch in range(COL_CHUNKS):
-        for d in range(1, n_col):
-            copy4(ch, d).wait_recv()
-
-        def finish_pair(i, carry, ch=ch):
-            hp = ch * per_col + i
-            for j in range(groups):
-                lanes = slice(j * LANES, (j + 1) * LANES)
-                lower, upper = swap_halves(
-                    recv4[ch, 2 * j, i].astype(f32), recv4[ch, 2 * j + 1, i].astype(f32)
-                )
-                patches[hp, :, lanes] = lower.astype(bf16)
-                patches[hp + pairs, :, lanes] = upper.astype(bf16)
-            return carry
-
-        lax.fori_loop(0, per_col, finish_pair, 0)
-        for side in range(2):
-            leave(ch, side).start()
+        if z > 0:
+            finish(z - 1)
+
+    finish(zc - 1)
 
     for ch in range(COL_CHUNKS):
         for d in range(1, n_col):
@@ -643,7 +654,7 @@
         depth_kernel,
         *[jnp.asarray(t) for t in tables],
     )
-    branches = pl.pallas_call(
+    return pl.pallas_call(
         functools.partial(
             mixing_kernel, n_row, n_col, exact_scale(grid_w)[1], exact_scale(grid_h)[1]
         ),
@@ -684,7 +695,6 @@
         ),
         cost_estimate=pl.CostEstimate(flops=2_000_000_000, bytes_accessed=3_000_000, transcendentals=600_000),
     )(*operands)
-    return (patches.astype(f32) + branches.astype(f32)).astype(bf16)
 
 
 def fits(patches, w_first):

time: 73.5 us -> 73 us (level)
  other arithmetic: 2.61 us -> 0 us
  local copies, waits for them, and re-layouts: 0.01 us -> 2.3 us
    convert_element_type x1 -> x0, other arithmetic: 2.61 us -> none  [fused(): return (patches.astype(f32) + branches.astype(f32)).astype(bf16)]
    unnamed x2 -> x1, local copies, waits for them, and re-layouts: 0.01 us -> 2.3 us
where the time goes in v5:
time: 73 us; the launch traced here: 72.9 us
  Pallas kernels  70.6 us (97%)
  local copies, waits for them, and re-layouts  2.3 us (3%)
    pallas_call x1, Pallas kernels, fused(): pl.pallas_call(functools.partial(mixing_kernel, n_row, n_col, exact_scale...  70.6 us
    unnamed x1, local copies, waits for them, and re-layouts  2.3 us

profile of v5, /device:TPU:0, one launch (start us, length us, event | category | flops | bytes accessed | tf_op | source)
XLA Modules:
  0.0 72.9 jit_solution(6966610797892278127)
XLA Ops:
  0.0 70.6 %shard_map.91 = bf16[32,64,256]{2,1,0:T(8,128)(2,1)} custom-call(bf16[32,64,256]{2,1,0:T(8,128)(2,1)} %patches_hbm.1, f32[1,256]{1,0:T(1,128)} %bitcast.1, bf16[2,4,64,64]{3,2,1,0:T(8,128)(2,1)} %w_first_hbm.1, bf16[2,4,64,64]{3,2,1,0:T(8,128)(2,1)} %w_second_hbm.1, f32[3,3,256]{2,1,0:T(4,128)} %depth_hbm.1, bf16[256,256]{1,0:T(8,128)(2,1)} %constant.8.clone.forward_hbm, ...), custom_call_target="tpu_custom_call" | custom-call | flops 2000000000 | bytes 3000000 | tf_op jit(solution)/shard_map/pallas_call | solution.py:657
  70.6 2.3 %copy.11 = bf16[32,64,256]{2,1,0:T(8,128)(2,1)} copy(bf16[32,64,256]{2,1,0:T(8,128)(2,1)} %shard_map.91) | data formatting | bytes 2097152

commit v6 on v5

--- a/solution.py
+++ b/solution.py
@@ -145,7 +145,7 @@
 SLOTS = 8
 TURN = 32
 COL_CHUNKS = 4
-KGROUPS = 2
+KGROUPS = 4
 BATCH = 2
 
 
@@ -360,8 +360,14 @@
             device_id_type=pl.DeviceIdType.MESH,
         )
 
+    def part_of(g, in_parts):
+        return pl.ds(g * per_k, per_k) if in_parts else pl.ds(0, kl // 2)
+
+    parts2 = [KGROUPS if z == zc - 1 else 1 for z in range(zc)]
+    parts3 = [KGROUPS if z == 0 else 1 for z in range(zc)]
+
     def copy2(z, g, d):
-        ks = pl.ds(g * per_k, per_k)
+        ks = part_of(g, z == zc - 1)
         return pltpu.make_async_remote_copy(
             src_ref=send2.at[z, row_peer(d), ks],
             dst_ref=recv2.at[z, row, ks],
@@ -372,7 +378,7 @@
         )
 
     def copy3(z, g, d):
-        ks = pl.ds(g * per_k, per_k)
+        ks = part_of(g, z == 0)
         return pltpu.make_async_remote_copy(
             src_ref=send3.at[z, row_peer(d), ks],
             dst_ref=recv3.at[z, row, ks],
@@ -451,7 +457,7 @@
         swapped = dot(swap_ref[0], jnp.concatenate(tiles, axis=1)).astype(bf16)
         for own, part in zip(owners, lane_groups(swapped)):
             send2[z, own] = part.reshape(TURN // kl, kl // 2, TILE, LANES)
-        for g in range(KGROUPS):
+        for g in range(parts2[z]):
             for d in row_order_of:
                 copy2(z, g, d).start()
         recv2[z, row] = send2[z, row]
@@ -542,15 +548,14 @@
 
     for g in range(KGROUPS):
         for z in range(zc):
-            for d in range(1, n_row):
+            for d in range(1, n_row) if g < parts2[z] else ():
                 copy2(z, g, d).wait_recv()
         lax.fori_loop(g * per_k // BATCH, (g + 1) * per_k // BATCH, filter_modes, 0)
         for d in row_order_of:
             copy3(0, g, d).start()
     for z in range(1, zc):
-        for g in range(KGROUPS):
-            for d in row_order_of:
-                copy3(z, g, d).start()
+        for d in row_order_of:
+            copy3(z, 0, d).start()
     for z in range(zc):
         recv3[z, row] = send3[z, row]
 
@@ -589,7 +594,7 @@
             leave(ch, side).start()
 
     for z in range(zc):
-        for g in range(KGROUPS):
+        for g in range(parts3[z]):
             for d in range(1, n_row):
                 copy3(z, g, d).wait_recv()
 
@@ -618,9 +623,10 @@
             copy1(ch, d).wait_send()
             copy4(ch, d).wait_send()
     for z in range(zc):
-        for g in range(KGROUPS):
-            for d in range(1, n_row):
+        for d in range(1, n_row):
+            for g in range(parts2[z]):
                 copy2(z, g, d).wait_send()
+            for g in range(parts3[z]):
                 copy3(z, g, d).wait_send()
     for side in range(2):
         copy_rim(side).wait_send()

time: 73 us -> 72.7 us (level)
  no operation moved by 1% of the time
where the time goes in v6:
time: 72.7 us; the launch traced here: 72.6 us
  Pallas kernels  70.3 us (97%)
  local copies, waits for them, and re-layouts  2.3 us (3%)
    pallas_call x1, Pallas kernels, fused(): pl.pallas_call(functools.partial(mixing_kernel, n_row, n_col, exact_scale...  70.3 us
    unnamed x1, local copies, waits for them, and re-layouts  2.3 us

profile of v6, /device:TPU:0, one launch (start us, length us, event | category | flops | bytes accessed | tf_op | source)
XLA Modules:
  0.0 72.6 jit_solution(12531547507987804419)
XLA Ops:
  0.0 70.3 %shard_map.91 = bf16[32,64,256]{2,1,0:T(8,128)(2,1)} custom-call(bf16[32,64,256]{2,1,0:T(8,128)(2,1)} %patches_hbm.1, f32[1,256]{1,0:T(1,128)} %bitcast.1, bf16[2,4,64,64]{3,2,1,0:T(8,128)(2,1)} %w_first_hbm.1, bf16[2,4,64,64]{3,2,1,0:T(8,128)(2,1)} %w_second_hbm.1, f32[3,3,256]{2,1,0:T(4,128)} %depth_hbm.1, bf16[256,256]{1,0:T(8,128)(2,1)} %constant.8.clone.forward_hbm, ...), custom_call_target="tpu_custom_call" | custom-call | flops 2000000000 | bytes 3000000 | tf_op jit(solution)/shard_map/pallas_call | solution.py:663
  70.3 2.3 %copy.11 = bf16[32,64,256]{2,1,0:T(8,128)(2,1)} copy(bf16[32,64,256]{2,1,0:T(8,128)(2,1)} %shard_map.91) | data formatting | bytes 2097152

commit v7 on v6

--- a/solution.py
+++ b/solution.py
@@ -323,9 +323,8 @@
         rows = chunk_rows(ch, side)
         return pltpu.make_async_copy(patches_hbm.at[rows], patches.at[rows], patch_sem.at[ch, side])
 
-    def leave(ch, side):
-        rows = chunk_rows(ch, side)
-        return pltpu.make_async_copy(patches.at[rows], out_hbm.at[rows], out_sem.at[ch, side])
+    def leave(ch):
+        return pltpu.make_async_copy(recv4.at[ch], out_hbm.at[ch], out_sem.at[ch])
 
     operands = (
         (gain_hbm, gain),
@@ -576,22 +575,7 @@
         for d in range(1, n_col):
             copy4(ch, d).wait_recv()
 
-        def finish_pair(i, carry):
-            hp = ch * per_col + i
-            for j in range(groups):
-                lanes = slice(j * LANES, (j + 1) * LANES)
-                lower, upper = swap_halves(
-                    recv4[ch, 2 * j, i].astype(f32), recv4[ch, 2 * j + 1, i].astype(f32)
-                )
-                patches[hp, :, lanes] = (patches[hp, :, lanes].astype(f32) + lower).astype(bf16)
-                patches[hp + pairs, :, lanes] = (
-                    patches[hp + pairs, :, lanes].astype(f32) + upper
-                ).astype(bf16)
-            return carry
-
-        lax.fori_loop(0, per_col, finish_pair, 0, unroll=2)
-        for side in range(2):
-            leave(ch, side).start()
+        leave(ch).start()
 
     for z in range(zc):
         for g in range(parts3[z]):
@@ -631,8 +615,20 @@
     for side in range(2):
         copy_rim(side).wait_send()
     for ch in range(COL_CHUNKS):
-        for side in range(2):
-            leave(ch, side).wait()
+        leave(ch).wait()
+
+
+def finish_kernel(patches, branches, out):
+    f32 = jnp.float32
+    for i in range(patches.shape[1]):
+        for j in range(patches.shape[3] // LANES):
+            lanes = slice(j * LANES, (j + 1) * LANES)
+            both = swap_halves(
+                branches[0, 2 * j, i].astype(f32), branches[0, 2 * j + 1, i].astype(f32)
+            )
+            for side in range(2):
+                total = patches[side, i, :, lanes].astype(f32) + both[side]
+                out[side, i, :, lanes] = total.astype(out.dtype)
 
 
 def fused(patches, norm_gain, w_first, w_second, depth_kernel):
@@ -660,11 +656,11 @@
         depth_kernel,
         *[jnp.asarray(t) for t in tables],
     )
-    return pl.pallas_call(
+    branches = pl.pallas_call(
         functools.partial(
             mixing_kernel, n_row, n_col, exact_scale(grid_w)[1], exact_scale(grid_h)[1]
         ),
-        out_shape=jax.ShapeDtypeStruct(patches.shape, bf16),
+        out_shape=jax.ShapeDtypeStruct((COL_CHUNKS, n_col, per_col, cols_dev, LANES), bf16),
         in_specs=[anywhere] * 9,
         out_specs=anywhere,
         scratch_shapes=[
@@ -694,13 +690,26 @@
             rim_sems,
             pltpu.SemaphoreType.DMA((8,)),
             pltpu.SemaphoreType.DMA((COL_CHUNKS, 2)),
-            pltpu.SemaphoreType.DMA((COL_CHUNKS, 2)),
+            pltpu.SemaphoreType.DMA((COL_CHUNKS,)),
         ],
         compiler_params=pltpu.CompilerParams(
             collective_id=0, has_side_effects=True, vmem_limit_bytes=62 * 1024 * 1024
         ),
         cost_estimate=pl.CostEstimate(flops=2_000_000_000, bytes_accessed=3_000_000, transcendentals=600_000),
     )(*operands)
+    cells = pl.BlockSpec((2, per_col, cols_dev, chans), lambda ch: (0, ch, 0, 0))
+    sides = (2, pairs, cols_dev, chans)
+    mixed = pl.pallas_call(
+        finish_kernel,
+        grid=(COL_CHUNKS,),
+        out_shape=jax.ShapeDtypeStruct(sides, bf16),
+        in_specs=[
+            cells,
+            pl.BlockSpec((1, n_col, per_col, cols_dev, LANES), lambda ch: (ch, 0, 0, 0, 0)),
+        ],
+        out_specs=cells,
+    )(patches.reshape(sides), branches)
+    return mixed.reshape(patches.shape)
 
 
 def fits(patches, w_first):

time: 72.7 us -> 74.1 us (1.019)
  Pallas kernels: 70.3 us -> 73.9 us
  local copies, waits for them, and re-layouts: 2.3 us -> 0 us
    pallas_call x0 -> x1, Pallas kernels: none -> 3.87 us  [fused(): pl.pallas_call(finish_kernel, grid=(COL_CHUNKS,), out_shape=jax.ShapeDtyp...]
    unnamed x1 -> x0, local copies, waits for them, and re-layouts: 2.3 us -> none
where the time goes in v7:
time: 74.1 us; the launch traced here: 73.9 us
  Pallas kernels  73.9 us (100%)
    pallas_call x1, Pallas kernels, fused(): pl.pallas_call(functools.partial(mixing_kernel, n_row, n_col, exact_scale...  70 us
    pallas_call x1, Pallas kernels, fused(): pl.pallas_call(finish_kernel, grid=(COL_CHUNKS,), out_shape=jax.ShapeDtyp...  3.87 us

profile of v7, /device:TPU:0, one launch (start us, length us, event | category | flops | bytes accessed | tf_op | source)
XLA Modules:
  0.0 73.9 jit_solution(10481192787200306769)
XLA Ops:
  0.0 70.0 %shard_map.91.branches = bf16[4,4,4,64,128]{4,3,2,1,0:T(8,128)(2,1)} custom-call(bf16[32,64,256]{2,1,0:T(8,128)(2,1)} %patches_hbm.1, f32[1,256]{1,0:T(1,128)} %bitcast.4, bf16[2,4,64,64]{3,2,1,0:T(8,128)(2,1)} %w_first_hbm.1, bf16[2,4,64,64]{3,2,1,0:T(8,128)(2,1)} %w_second_hbm.1, f32[3,3,256]{2,1,0:T(4,128)} %depth_hbm.1, ...), custom_call_target="tpu_custom_call" | custom-call | flops 2000000000 | bytes 3000000 | tf_op jit(solution)/shard_map/pallas_call | solution.py:659
  70.0 3.9 %shard_map.92 = bf16[2,16,64,256]{3,2,1,0:T(8,128)(2,1)} custom-call(bf16[2,16,64,256]{3,2,1,0:T(8,128)(2,1)} %bitcast.3, bf16[4,4,4,64,128]{4,3,2,1,0:T(8,128)(2,1)} %shard_map.91.branches), custom_call_target="tpu_custom_call" | custom-call | tf_op jit(solution)/shard_map/pallas_call | solution.py:702

commit v8 on v6

--- a/solution.py
+++ b/solution.py
@@ -294,12 +294,7 @@
             bits, weight = bits // 2, 2 * weight
         return peer
 
-    near = list(range(1, n_row // 2))
-    row_order_of = []
-    for d in range(n_row // 2, n_row):
-        row_order_of.append(d)
-        if near:
-            row_order_of.append(near.pop(0))
+    row_order_of = list(range(n_row - 1, 0, -1))
 
     def to_col(d):
         return {"col": col_peer(d)}

time: 72.7 us -> 73.6 us (1.012)
  Pallas kernels: 70.3 us -> 71.1 us
    pallas_call x1, Pallas kernels: 70.3 us -> 71.1 us  [fused(): pl.pallas_call(functools.partial(mixing_kernel, n_row, n_col, exact_scale...]
where the time goes in v8:
time: 73.6 us; the launch traced here: 73.4 us
  Pallas kernels  71.1 us (97%)
  local copies, waits for them, and re-layouts  2.3 us (3%)
    pallas_call x1, Pallas kernels, fused(): pl.pallas_call(functools.partial(mixing_kernel, n_row, n_col, exact_scale...  71.1 us
    unnamed x1, local copies, waits for them, and re-layouts  2.3 us

profile of v8, /device:TPU:0, one launch (start us, length us, event | category | flops | bytes accessed | tf_op | source)
XLA Modules:
  0.0 73.4 jit_solution(1382708018773425916)
XLA Ops:
  0.0 71.1 %shard_map.91 = bf16[32,64,256]{2,1,0:T(8,128)(2,1)} custom-call(bf16[32,64,256]{2,1,0:T(8,128)(2,1)} %patches_hbm.1, f32[1,256]{1,0:T(1,128)} %bitcast.1, bf16[2,4,64,64]{3,2,1,0:T(8,128)(2,1)} %w_first_hbm.1, bf16[2,4,64,64]{3,2,1,0:T(8,128)(2,1)} %w_second_hbm.1, f32[3,3,256]{2,1,0:T(4,128)} %depth_hbm.1, bf16[256,256]{1,0:T(8,128)(2,1)} %constant.8.clone.forward_hbm, ...), custom_call_target="tpu_custom_call" | custom-call | flops 2000000000 | bytes 3000000 | tf_op jit(solution)/shard_map/pallas_call | solution.py:658
  71.1 2.3 %copy.11 = bf16[32,64,256]{2,1,0:T(8,128)(2,1)} copy(bf16[32,64,256]{2,1,0:T(8,128)(2,1)} %shard_map.91) | data formatting | bytes 2097152
